TPU v7x, 32 devices: a whole 2x2x4 slice. The times are simulated.
32 devices in a mesh: fsdp: 8 (over y, x, core), tp: 4 (over z).
Axes of the slice: x: 2, y: 2, z: 4, core: 2. Of those that a mesh axis runs over, the one named last changes fastest.
Arguments:
- tokens: bfloat16 [8, 1024, 2048], P('fsdp', 'tp'), may hold values from -6 to 6
- layer_norm_gain: float32 [2048], replicated, may hold values from 0.25 to 1.75
- layer_norm_bias: float32 [2048], replicated, may hold values from -3 to 3
- w_qkv: bfloat16 [2048, 3, 2048], P('fsdp', None, 'tp'), may hold values from -0.125 to 0.125
- w_out: bfloat16 [2048, 2048], P('tp', 'fsdp'), may hold values from -0.75 to 0.75
- w_up: bfloat16 [2048, 8192], P('fsdp', 'tp'), may hold values from -0.125 to 0.125
- w_down: bfloat16 [8192, 2048], P('tp', 'fsdp'), may hold values from -0.0625 to 0.0625
- cotangent: bfloat16 [8, 1024, 2048], P('fsdp', 'tp'), may hold values from -6 to 6
Outputs:
- output: bfloat16 [8, 1024, 2048], P('fsdp', 'tp')
- in_grad: float32 [8, 1024, 2048], P('fsdp', 'tp')
- gain_grad: float32 [2048], P('fsdp')
- bias_grad: float32 [2048], P('fsdp')
- qkv_grad: float32 [2048, 3, 2048], P('fsdp', None, 'tp')
- out_grad: float32 [2048, 2048], P('tp', 'fsdp')
- up_grad: float32 [2048, 8192], P('fsdp', 'tp')
- down_grad: float32 [8192, 2048], P('tp', 'fsdp')
All inputs are finite; a program needn't handle non-finite values.
Results may differ from a plain program's by a relative error of at most 0.012.
Values may be sent and summed in bfloat16 or wider, within the bound.
No kernel may reach another device: no remote copies, remote signals or barrier semaphores. Data moves between devices by JAX's collectives and lax.ppermute only.
A program may use at most 256 MiB of HBM per device.

v0:
```python
import jax
import jax.numpy as jnp
from jax import lax
from jax.sharding import PartitionSpec as P

HEADS = 32
HEAD_DIM = 64
ROT = 32


def angle_tables(length):
    half_rot = ROT // 2
    position = jnp.arange(length, dtype=jnp.int32).astype(jnp.float32)[:, None]
    channel = jnp.arange(HEAD_DIM, dtype=jnp.int32)
    exponent = (2 * (channel % half_rot)).astype(jnp.float32) / ROT
    angles = position * (10000.0 ** (-exponent))[None, :]
    inside = (channel < ROT)[None, :]
    return (jnp.where(inside, jnp.cos(angles), 1.0), jnp.where(inside, jnp.sin(angles), 0.0))


def turn_half(vectors):
    half_rot = ROT // 2
    return jnp.concatenate(
        [-vectors[..., half_rot:ROT], vectors[..., :half_rot], vectors[..., ROT:]], axis=-1
    )


def turn_back(vectors):
    half_rot = ROT // 2
    return jnp.concatenate(
        [vectors[..., half_rot:ROT], -vectors[..., :half_rot], vectors[..., ROT:]], axis=-1
    )


def rotate(vectors, cosine_tab, sine_tab):
    return vectors * cosine_tab[None, :, None, :] + turn_half(vectors) * sine_tab[None, :, None, :]


def rotate_back(vectors, cosine_tab, sine_tab):
    return vectors * cosine_tab[None, :, None, :] + turn_back(vectors * sine_tab[None, :, None, :])


def causal_scores(query_rows, key_rows, start):
    scores = jnp.einsum(
        "qhd,khd->hqk", query_rows, key_rows, preferred_element_type=jnp.float32
    ) * HEAD_DIM ** (-0.5)
    row_pos = start + jnp.arange(query_rows.shape[0], dtype=jnp.int32)
    col_pos = jnp.arange(key_rows.shape[0], dtype=jnp.int32)
    allowed = col_pos[None, None, :] <= row_pos[None, :, None]
    return jnp.where(allowed, scores, -1e30)


def attend_forward(operands):
    queries, key_rows, value_rows = operands
    length = queries.shape[0]
    block_rows = min(512, length)
    outputs = []
    totals = []
    for block_idx in range(length // block_rows):
        start = block_idx * block_rows
        finish = start + block_rows
        scores = causal_scores(queries[start:finish], key_rows[:finish], start)
        largest = jnp.max(scores, axis=-1, keepdims=True)
        exp_terms = jnp.exp(scores - largest)
        row_total = jnp.sum(exp_terms, axis=-1, keepdims=True)
        prob_rows = (exp_terms / row_total).astype(jnp.bfloat16)
        block_out = jnp.einsum(
            "hqk,khd->qhd", prob_rows, value_rows[:finish], preferred_element_type=jnp.float32
        )
        outputs.append(block_out.astype(jnp.bfloat16))
        totals.append((largest + jnp.log(row_total))[..., 0])
    return (jnp.concatenate(outputs, axis=0), jnp.concatenate(totals, axis=1))


def attend_backward(operands):
    queries, key_rows, value_rows, d_out, log_total = operands
    length = queries.shape[0]
    block_rows = min(512, length)
    scale = HEAD_DIM ** (-0.5)
    key_grad = jnp.zeros(key_rows.shape, jnp.float32)
    value_grad = jnp.zeros(value_rows.shape, jnp.float32)
    query_grads = []
    for block_idx in range(length // block_rows):
        start = block_idx * block_rows
        finish = start + block_rows
        query_rows = queries[start:finish]
        grad_rows = d_out[start:finish]
        scores = causal_scores(query_rows, key_rows[:finish], start)
        prob_rows = jnp.exp(scores - log_total[:, start:finish, None])
        d_prob = jnp.einsum(
            "qhd,khd->hqk", grad_rows, value_rows[:finish], preferred_element_type=jnp.float32
        )
        centre = jnp.sum(prob_rows * d_prob, axis=-1, keepdims=True)
        d_scores = (prob_rows * (d_prob - centre)).astype(jnp.bfloat16)
        query_grads.append(
            jnp.einsum(
                "hqk,khd->qhd", d_scores, key_rows[:finish], preferred_element_type=jnp.float32
            )
            * scale
        )
        key_grad = key_grad.at[:finish].add(
            jnp.einsum("hqk,qhd->khd", d_scores, query_rows, preferred_element_type=jnp.float32)
            * scale
        )
        value_grad = value_grad.at[:finish].add(
            jnp.einsum(
                "hqk,qhd->khd",
                prob_rows.astype(jnp.bfloat16),
                grad_rows,
                preferred_element_type=jnp.float32,
            )
        )
    return (jnp.concatenate(query_grads, axis=0), key_grad, value_grad)


def gelu_tanh(values_in):
    return jax.nn.gelu(values_in, approximate=True)


def local(tokens, layer_norm_gain, layer_norm_bias, w_qkv, w_out, w_up, w_down, cotangent):
    seq_count, own_rows, width = tokens.shape
    groups = lax.axis_size("tp")
    heads_here = HEADS // groups
    local_width = heads_here * HEAD_DIM
    length = own_rows * groups
    token_total = seq_count * length
    tokens_f = tokens.astype(jnp.float32)
    average = jnp.mean(tokens_f, axis=-1, keepdims=True)
    mean_removed = tokens_f - average
    input_variance = jnp.mean(mean_removed * mean_removed, axis=-1, keepdims=True)
    inverse_scale = lax.rsqrt(input_variance + 1e-05)
    standardized_input = mean_removed * inverse_scale
    norm_output = (standardized_input * layer_norm_gain + layer_norm_bias).astype(jnp.bfloat16)
    gathered = lax.all_gather(norm_output, "tp", axis=1, tiled=True)
    flat_normed = gathered.reshape(token_total, width)
    full_qkv, full_out, full_up, full_down = (
        lax.all_gather(w_qkv, "fsdp", axis=0, tiled=True),
        lax.all_gather(w_out, "fsdp", axis=1, tiled=True),
        lax.all_gather(w_up, "fsdp", axis=0, tiled=True),
        lax.all_gather(w_down, "fsdp", axis=1, tiled=True),
    )
    qkv_raw = jnp.dot(
        flat_normed, full_qkv.reshape(width, 3 * local_width), preferred_element_type=jnp.float32
    )
    qkv_raw = qkv_raw.reshape(seq_count, length, 3, heads_here, HEAD_DIM)
    cosine_tab, sine_tab = angle_tables(length)
    queries = rotate(qkv_raw[:, :, 0], cosine_tab, sine_tab).astype(jnp.bfloat16)
    key_rows = rotate(qkv_raw[:, :, 1], cosine_tab, sine_tab).astype(jnp.bfloat16)
    value_rows = qkv_raw[:, :, 2].astype(jnp.bfloat16)
    attended, log_total = lax.map(attend_forward, (queries, key_rows, value_rows))
    attended_flat = attended.reshape(token_total, local_width)
    up_proj = jnp.dot(flat_normed, full_up, preferred_element_type=jnp.float32)
    hidden = gelu_tanh(up_proj).astype(jnp.bfloat16)
    branch_part = jnp.dot(attended_flat, full_out, preferred_element_type=jnp.float32)
    branch_part = branch_part + jnp.dot(hidden, full_down, preferred_element_type=jnp.float32)
    summed = lax.psum_scatter(
        branch_part.reshape(seq_count, length, width), "tp", scatter_dimension=1, tiled=True
    )
    output = (tokens_f + summed).astype(jnp.bfloat16)
    cot_rows = lax.all_gather(cotangent, "tp", axis=1, tiled=True).reshape(token_total, width)
    grad_out = jnp.einsum("tk,td->kd", attended_flat, cot_rows, preferred_element_type=jnp.float32)
    grad_down = jnp.einsum("tf,td->fd", hidden, cot_rows, preferred_element_type=jnp.float32)
    d_att = jnp.einsum("td,kd->tk", cot_rows, full_out, preferred_element_type=jnp.float32).astype(
        jnp.bfloat16
    )
    d_hidden = jnp.einsum("td,fd->tf", cot_rows, full_down, preferred_element_type=jnp.float32)
    gelu_pull = jax.vjp(gelu_tanh, up_proj)[1]
    d_up = gelu_pull(d_hidden)[0].astype(jnp.bfloat16)
    grad_up = jnp.einsum("tw,tf->wf", flat_normed, d_up, preferred_element_type=jnp.float32)
    d_att_heads = d_att.reshape(seq_count, length, heads_here, HEAD_DIM)
    d_query, d_key, d_value = lax.map(
        attend_backward, (queries, key_rows, value_rows, d_att_heads, log_total)
    )
    d_qkv = (
        jnp.stack(
            [
                rotate_back(d_query, cosine_tab, sine_tab),
                rotate_back(d_key, cosine_tab, sine_tab),
                d_value,
            ],
            axis=2,
        )
        .astype(jnp.bfloat16)
        .reshape(token_total, 3 * local_width)
    )
    grad_qkv = jnp.einsum("tw,tc->wc", flat_normed, d_qkv, preferred_element_type=jnp.float32)
    grad_qkv = grad_qkv.reshape(width, 3, local_width)
    norm_part = jnp.einsum(
        "tc,wc->tw",
        d_qkv,
        full_qkv.reshape(width, 3 * local_width),
        preferred_element_type=jnp.float32,
    )
    norm_part = norm_part + jnp.einsum(
        "tf,wf->tw", d_up, full_up, preferred_element_type=jnp.float32
    )
    norm_output_gradient = lax.psum_scatter(
        norm_part.reshape(seq_count, length, width), "tp", scatter_dimension=1, tiled=True
    )
    gain_contribution = jnp.sum(norm_output_gradient * standardized_input, axis=(0, 1))
    bias_part = jnp.sum(norm_output_gradient, axis=(0, 1))
    norm_stats = jnp.stack([gain_contribution, bias_part], axis=0)
    normalized_gradient = norm_output_gradient * layer_norm_gain
    in_grad = cotangent.astype(jnp.float32) + inverse_scale * (
        normalized_gradient
        - jnp.mean(normalized_gradient, axis=-1, keepdims=True)
        - standardized_input
        * jnp.mean(normalized_gradient * standardized_input, axis=-1, keepdims=True)
    )
    grad_qkv, grad_out, grad_up, grad_down, norm_stats = (
        lax.psum_scatter(grad_qkv, "fsdp", scatter_dimension=0, tiled=True),
        lax.psum_scatter(grad_out, "fsdp", scatter_dimension=1, tiled=True),
        lax.psum_scatter(grad_up, "fsdp", scatter_dimension=0, tiled=True),
        lax.psum_scatter(grad_down, "fsdp", scatter_dimension=1, tiled=True),
        lax.psum_scatter(norm_stats, "fsdp", scatter_dimension=1, tiled=True),
    )
    norm_stats = lax.psum(norm_stats, "tp")
    return (output, in_grad, norm_stats[0], norm_stats[1], grad_qkv, grad_out, grad_up, grad_down)


def solution(mesh):
    return jax.shard_map(
        local,
        mesh=mesh,
        in_specs=(
            P("fsdp", "tp", None),
            P(),
            P(),
            P("fsdp", None, "tp"),
            P("tp", "fsdp"),
            P("fsdp", "tp"),
            P("tp", "fsdp"),
            P("fsdp", "tp", None),
        ),
        out_specs=(
            P("fsdp", "tp", None),
            P("fsdp", "tp", None),
            P("fsdp"),
            P("fsdp"),
            P("fsdp", None, "tp"),
            P("tp", "fsdp"),
            P("fsdp", "tp"),
            P("tp", "fsdp"),
        ),
        check_vma=False,
    )
```

profile of v0, /device:TPU:0, one launch (start us, length us, event | category | flops | bytes accessed | tf_op | source)
XLA Modules:
  0.0 1136.4 jit_solution(3159164944063536263)
XLA Ops:
  8.7 1.4 convert_reduce_fusion
  10.2 1.6 fusion.53
  12.4 2.7 fusion.47
  20.5 20.3 %all-gather.11.cloned.1.call-done = bf16[512,2048]{1,0:T(8,128)(2,1)} async-done(((bf16[512,256]{1,0:T(8,128)(2,1)}), bf16[512,2048]{1,0:T(8,128)(2,1)}) %all-gather.11.cloned.1.call-update) | async-done | bytes 2097168 | tf_op jit(solution)/shard_map/all_gather | solution.py:138
  40.8 82.4 %all-gather.17.cloned.1.call-done = bf16[1,1024,2048]{2,1,0:T(8,128)(2,1)} async-done(((bf16[1,256,2048]{2,1,0:T(8,128)(2,1)}), bf16[1,1024,2048]{2,1,0:T(8,128)(2,1)}) %all-gather.17.cloned.1.call-update) | async-done | bytes 4194320 | tf_op jit(solution)/shard_map/all_gather | solution.py:160
  123.2 5.2 fusion.67
  129.3 75.4 %all-gather.7.cloned.1.call-done = bf16[1,1024,2048]{2,1,0:T(8,128)(2,1)} async-done(((bf16[1,256,2048]{2,1,0:T(8,128)(2,1)}), bf16[1,1024,2048]{2,1,0:T(8,128)(2,1)}) %all-gather.7.cloned.1.call-update) | async-done | bytes 4194320 | tf_op jit(solution)/shard_map/all_gather | solution.py:134
  204.7 47.5 %all-gather.9.cloned.1.call-done = bf16[2048,3,512]{0,2,1:T(8,128)(2,1)} async-done(((bf16[256,3,512]{0,2,1:T(8,128)(2,1)}), bf16[2048,3,512]{0,2,1:T(8,128)(2,1)}) %all-gather.9.cloned.1.call-update) | async-done | bytes 6291472 | tf_op jit(solution)/shard_map/all_gather | solution.py:137
  252.2 10.2 fusion.37
  264.8 1.5 fusion.109
  268.9 3.1 fusion.108
  272.1 4.0 fusion
  276.1 1.7 copy-done
  277.8 1.7 fusion.103
  279.6 1.9 multiply_reduce_fusion.1
  281.5 2.6 multiply_convert_fusion.1
  284.9 12.1 %multiply_reduce_fusion = (f32[8,512]{1,0:T(8,128)S(1)}, f32[8,512,1024]{2,1,0:T(8,128)}) fusion(f32[8,512,1024]{2,1,0:T(8,128)} %copy-done, f32[8,512]{1,0:T(8,128)S(1)} %log_add_fusion, bf16[512,8,64]{0,2,1:T(8,128)(2,1)S(1)} %bitcast.201, f32[1,1024,3,8,64]{1,4,3,2,0:T(8,128)} %copy-done.3), kind=kOutput, calls=%fused_computation.1 | convolution fusion | flops 549449728 | bytes 35160064 | tf_op jit(solution)/shard_map/while/body/eval_jaxpr/qhd,khd->hqk/dot_general | solution.py:90
  297.0 12.0 %multiply_convert_fusion = bf16[8,512,1024]{2,1,0:T(8,128)(2,1)S(1)} fusion(f32[8,512,1024]{2,1,0:T(8,128)} %get-tuple-element.176, f32[8,512,1024]{2,1,0:T(8,128)} %copy-done, f32[8,512]{1,0:T(8,128)S(1)} %get-tuple-element.175, f32[8,512]{1,0:T(8,128)S(1)} %log_add_fusion), kind=kLoop, calls=%fused_computation | loop fusion | flops 16777216 | bytes 41975808 | tf_op jit(solution)/shard_map/while/body/eval_jaxpr/convert_element_type | solution.py:94
  309.0 2.7 convolution_multiply_fusion.2
  312.9 1.5 fusion.88
  315.8 1.6 bitcast_add_fusion.1
  317.8 1.5 fusion.81
  320.1 1.4 fusion.73
  324.5 3.0 fusion.70
  327.5 3.1 pad_maximum_fusion
  330.6 14.8 %fusion.29 = f32[1024,2048]{1,0:T(8,128)} fusion(bf16[2048,2048]{1,0:T(8,128)(2,1)} %all-gather.13.cloned.1.call-done, bf16[1,1024,2048]{2,1,0:T(8,128)(2,1)} %all-gather.7.cloned.1.call-done), kind=kOutput, calls=%fused_computation.44 | convolution fusion | flops 8589934592 | bytes 20971520 | tf_op jit(solution)/shard_map/dot_general | solution.py:152
  345.4 20.7 %all-gather.15.cloned.1.call-done = bf16[2048,2048]{1,0:T(8,128)(2,1)} async-done(((bf16[2048,256]{1,0:T(8,128)(2,1)}), bf16[2048,2048]{1,0:T(8,128)(2,1)}) %all-gather.15.cloned.1.call-update) | async-done | bytes 8388624 | tf_op jit(solution)/shard_map/all_gather | solution.py:140
  366.1 18.3 %fusion.8 = bf16[1024,2048]{1,0:T(8,128)(2,1)S(1)} fusion(f32[1024,2048]{1,0:T(8,128)} %fusion.29, bf16[2048,2048]{1,0:T(8,128)(2,1)} %all-gather.15.cloned.1.call-done, bf16[1,1024,2048]{2,1,0:T(8,128)(2,1)} %all-gather.17.cloned.1.call-done), kind=kOutput, calls=%fused_computation.16 | convolution fusion | flops 8631877632 | bytes 25165824 | tf_op jit(solution)/shard_map/td,fd->tf/dot_general | solution.py:166
  384.5 8.8 fusion.110
  393.3 10.8 add_bitcast_fusion
  405.4 5.0 fusion.80
  410.4 8.6 fusion.79
  419.2 12.0 %fusion.104 = f32[1024,2048]{1,0:T(8,128)S(1)} fusion(bf16[2048,2048]{1,0:T(8,128)(2,1)S(1)} %bitcast.213, f32[1024,2048]{1,0:T(8,128)} %fusion.29), kind=kOutput, calls=%fused_computation.165 | convolution fusion | flops 8608808960 | bytes 25165824 | tf_op jit(solution)/shard_map/dot_general | solution.py:155
  431.3 5.7 add_bitcast_fusion.1
  437.1 111.8 %reduce-scatter.12.cloned.1.call-done = f32[1,256,2048]{2,1,0:T(8,128)} async-done(((f32[1,1024,2048]{2,1,0:T(8,128)}), f32[1,256,2048]{2,1,0:T(8,128)}) %reduce-scatter.12.cloned.1.call-update) | async-done | bytes 2097168 | tf_op jit(solution)/shard_map/reduce_scatter | solution.py:197
  548.8 2.6 fusion.52
  552.9 6.5 fusion.23
  559.5 12.9 %fusion.17 = f32[2048,3,512]{2,0,1:T(8,128)} fusion(bf16[3,512,1024]{2,1,0:T(8,128)(2,1)} %bitcast.206, bf16[1,1024,2048]{2,1,0:T(8,128)(2,1)} %all-gather.7.cloned.1.call-done), kind=kOutput, calls=%fused_computation.32 | convolution fusion | flops 6442450944 | bytes 19922944 | tf_op jit(solution)/shard_map/tw,tc->wc/dot_general | solution.py:186
  572.4 16.7 %fusion.21 = f32[2048,2048]{1,0:T(8,128)} fusion(bf16[1,1024,2048]{2,1,0:T(8,128)(2,1)} %all-gather.17.cloned.1.call-done, f32[1024,2048]{1,0:T(8,128)} %fusion.29), kind=kOutput, calls=%fused_computation.36 | convolution fusion | flops 8608808960 | bytes 29360128 | tf_op jit(solution)/shard_map/tf,td->fd/dot_general | solution.py:162
  589.2 15.5 %fusion.31 = f32[2048,2048]{1,0:T(8,128)} fusion(bf16[1024,2048]{1,0:T(8,128)(2,1)} %copy-done.21, bf16[1,1024,2048]{2,1,0:T(8,128)(2,1)} %all-gather.7.cloned.1.call-done), kind=kOutput, calls=%fused_computation.46 | convolution fusion | flops 8589934592 | bytes 25165824 | tf_op jit(solution)/shard_map/tw,tf->wf/dot_general | solution.py:169
  604.7 91.7 %reduce-scatter.10.cloned.1.call-done = f32[1,256,2048]{2,1,0:T(8,128)} async-done(((f32[1,1024,2048]{2,1,0:T(8,128)}), f32[1,256,2048]{2,1,0:T(8,128)}) %reduce-scatter.10.cloned.1.call-update) | async-done | bytes 2097168 | tf_op jit(solution)/shard_map/reduce_scatter | solution.py:156
  696.4 4.5 fusion.51
  701.0 35.4 %reduce-scatter.22.cloned.1.call-done = f32[256,2]{1,0:T(8,128)} async-done(((f32[2048,2]{1,0:T(8,128)}), f32[256,2]{1,0:T(8,128)}) %reduce-scatter.22.cloned.1.call-update) | async-done | bytes 2064
  737.4 11.7 %psum.7 = f32[2,256]{1,0:T(2,128)S(1)} all-reduce(f32[2,256]{1,0:T(2,128)S(1)} %copy.41), channel_id=1, replica_groups=mesh['fsdp'=8,'tp'=4] {'tp'}, use_global_device_ids=true, to_apply=%region_15.16 | all-reduce | flops 512 | bytes 4096 | tf_op jit(solution)/shard_map/psum | solution.py:217
  749.7 41.9 %reduce-scatter.16.cloned.1.call-done = f32[512,256]{1,0:T(8,128)} async-done(((f32[512,2048]{1,0:T(8,128)}), f32[512,256]{1,0:T(8,128)}) %reduce-scatter.16.cloned.1.call-update) | async-done | bytes 524304 | tf_op jit(solution)/shard_map/reduce_scatter | solution.py:212
  791.5 96.9 %reduce-scatter.14.cloned.1.call-done = f32[256,3,512]{2,0,1:T(8,128)} async-done(((f32[2048,3,512]{2,0,1:T(8,128)}), f32[256,3,512]{2,0,1:T(8,128)}) %reduce-scatter.14.cloned.1.call-update) | async-done | bytes 1572880 | tf_op jit(solution)/shard_map/reduce_scatter | solution.py:211
  888.4 120.4 %reduce-scatter.20.cloned.1.call-done = f32[2048,256]{1,0:T(8,128)} async-done(((f32[2048,2048]{1,0:T(8,128)}), f32[2048,256]{1,0:T(8,128)}) %reduce-scatter.20.cloned.1.call-update) | async-done | bytes 2097168 | tf_op jit(solution)/shard_map/reduce_scatter | solution.py:214
  1008.8 120.5 %reduce-scatter.18.cloned.1.call-done = f32[256,2048]{1,0:T(8,128)} async-done(((f32[2048,2048]{1,0:T(8,128)}), f32[256,2048]{1,0:T(8,128)}) %reduce-scatter.18.cloned.1.call-update) | async-done | bytes 2097168 | tf_op jit(solution)/shard_map/reduce_scatter | solution.py:213
  (128 shorter events, 25.3 us)
Async XLA Ops:
  7.2 8.0 copy-start.13
  7.2 33.6 %all-gather.11.cloned.1.call-start = ((), (), s32[]{:S(2)}) async-start(), calls=%async_computation.9 | async-start | bytes 2359296 | tf_op jit(solution)/shard_map/all_gather | solution.py:138
  7.9 115.3 %all-gather.17.cloned.1.call-start = ((), (), s32[]{:S(2)}) async-start(), calls=%async_computation.13 | async-start | bytes 5242880 | tf_op jit(solution)/shard_map/all_gather | solution.py:160
  8.7 196.0 %all-gather.7.cloned.1.call-start = ((), (), s32[]{:S(2)}) async-start(), calls=%async_computation.7 | async-start | bytes 5242880 | tf_op jit(solution)/shard_map/all_gather | solution.py:134
  10.2 1.7 copy-start.16
  11.8 0.6 copy-start.18
  15.1 237.1 %all-gather.9.cloned.1.call-start = ((), (), s32[]{:S(2)}) async-start(), calls=%async_computation.8 | async-start | bytes 7077888 | tf_op jit(solution)/shard_map/all_gather | solution.py:137
  16.3 314.3 %all-gather.13.cloned.1.call-start = ((), (), s32[]{:S(2)}) async-start(), calls=%async_computation.10 | async-start | bytes 9437184 | tf_op jit(solution)/shard_map/all_gather | solution.py:139
  16.9 349.2 %all-gather.15.cloned.1.call-start = ((), (), s32[]{:S(2)}) async-start(), calls=%async_computation.11 | async-start | bytes 9437184 | tf_op jit(solution)/shard_map/all_gather | solution.py:140
  17.5 531.3 %reduce-scatter.12.cloned.1.call-start = ((), (), s32[]{:S(2)}) async-start(), calls=%async_computation.14 | async-start | bytes 10485760 | tf_op jit(solution)/shard_map/reduce_scatter | solution.py:197
  262.4 5.1 copy-start.3
  263.4 1.1 copy-start.14
  264.7 1.6 copy-start.7
  266.3 15.2 %copy-start.1 = (f32[8,512,512]{1,2,0:T(8,128)}, f32[8,512,512]{1,2,0:T(8,128)S(1)}, u32[]{:S(2)}) copy-start(f32[8,512,512]{1,2,0:T(8,128)S(1)} %get-tuple-element.172) | copy-start | bytes 25165828
  267.5 1.4 copy-start.12
  272.1 5.7 copy-start
  272.1 7.5 copy-start.5
  279.6 1.9 copy-start.9
  281.5 2.6 copy-start.8
  314.4 4.9 slice-start.4
  315.8 3.5 slice-start.5
  315.8 5.7 slice-start
  315.8 6.2 slice-start.1
  317.6 5.7 slice-start.2
  317.7 2.4 copy-start.6
  320.1 4.4 slice-start.3
  366.1 18.3 %copy-start.20 = (bf16[2048,2048]{1,0:T(8,128)(2,1)S(1)}, bf16[2048,2048]{1,0:T(8,128)(2,1)}, u32[]{:S(2)}) copy-start(bf16[2048,2048]{1,0:T(8,128)(2,1)} %all-gather.13.cloned.1.call-done) | copy-start | bytes 25165828
  384.5 8.9 copy-start.21
  404.2 1.2 copy-start.10
  404.2 292.2 %reduce-scatter.10.cloned.1.call-start = ((), (), s32[]{:S(2)}) async-start(), calls=%async_computation.12 | async-start | bytes 10485760 | tf_op jit(solution)/shard_map/reduce_scatter | solution.py:156
  405.4 13.8 %slice-start.6 = ((s8[8388608]{0:T(1024)(128)(4,1)}), s8[4194304]{0:T(1024)(128)(4,1)S(1)}, s32[]{:S(2)}) async-start(s8[8388608]{0:T(1024)(128)(4,1)} %bitcast.212), calls=%async_computation.26 | async-start | bytes 8388608
  410.4 8.8 slice-start.7
  419.2 12.0 %copy-start.11 = (bf16[512,2048]{1,0:T(8,128)(2,1)S(1)}, bf16[512,2048]{1,0:T(8,128)(2,1)}, u32[]{:S(2)}) copy-start(bf16[512,2048]{1,0:T(8,128)(2,1)} %all-gather.11.cloned.1.call-done) | copy-start | bytes 6291460
  437.0 111.9 %copy-start.2 = (bf16[1,256,2048]{2,1,0:T(8,128)(2,1)S(1)}, bf16[1,256,2048]{2,1,0:T(8,128)(2,1)}, u32[]{:S(2)}) copy-start(bf16[1,256,2048]{2,1,0:T(8,128)(2,1)} %param.20) | copy-start | bytes 3145732
  437.0 111.9 %copy-start.15 = (f32[2048]{0:T(1024)S(1)}, f32[2048]{0:T(1024)}, u32[]{:S(2)}) copy-start(f32[2048]{0:T(1024)} %param.21) | copy-start | bytes 24580
  437.0 111.9 %copy-start.17 = (f32[256]{0:T(256)S(1)}, f32[256]{0:T(256)}, u32[]{:S(2)}) copy-start(f32[256]{0:T(256)} %copy-done.16) | copy-start | bytes 3076
  437.0 111.9 %copy-start.19 = (f32[256]{0:T(256)S(1)}, f32[256]{0:T(256)}, u32[]{:S(2)}) copy-start(f32[256]{0:T(256)} %copy-done.18) | copy-start | bytes 3076
  437.0 299.4 %reduce-scatter.22.cloned.1.call-start = ((), (), s32[]{:S(2)}) async-start(), calls=%async_computation.19 | async-start | bytes 1179648
  552.9 238.7 %reduce-scatter.16.cloned.1.call-start = ((), (), s32[]{:S(2)}) async-start(), calls=%async_computation.16 | async-start | bytes 4718592 | tf_op jit(solution)/shard_map/reduce_scatter | solution.py:212
  559.4 329.0 %reduce-scatter.14.cloned.1.call-start = ((), (), s32[]{:S(2)}) async-start(), calls=%async_computation.15 | async-start | bytes 14155776 | tf_op jit(solution)/shard_map/reduce_scatter | solution.py:211
  572.4 436.5 %reduce-scatter.20.cloned.1.call-start = ((), (), s32[]{:S(2)}) async-start(), calls=%async_computation.18 | async-start | bytes 18874368 | tf_op jit(solution)/shard_map/reduce_scatter | solution.py:214
  589.2 540.2 %reduce-scatter.18.cloned.1.call-start = ((), (), s32[]{:S(2)}) async-start(), calls=%async_computation.17 | async-start | bytes 18874368 | tf_op jit(solution)/shard_map/reduce_scatter | solution.py:213
  604.7 91.7 %copy-start.4 = (f32[1,256,2048]{2,1,0:T(8,128)S(1)}, f32[1,256,2048]{2,1,0:T(8,128)}, u32[]{:S(2)}) copy-start(f32[1,256,2048]{2,1,0:T(8,128)} %reduce-scatter.12.cloned.1.call-done) | copy-start | bytes 6291460
Sparse Core Ops, SparseCore 0:
  9.9 30.8 all-gather.10
  42.4 80.7 all-gather.16
  125.3 79.2 all-gather.6
  207.0 45.1 all-gather.8
  253.9 54.3 all-gather.12
  310.1 56.0 all-gather.14
  404.3 144.4 reduce-scatter.11
  551.2 145.2 reduce-scatter.9
  699.6 36.7 reduce-scatter.21
  740.2 51.3 reduce-scatter.15
  796.0 92.3 reduce-scatter.13
  892.9 115.9 reduce-scatter.19
  1013.4 115.9 reduce-scatter.17
where the time goes:
time: 1140 us
  waiting for transfers between devices  867 us (76%)
  matrix products  181 us (16%)
  other arithmetic  44.3 us (4%)
  local copies, waits for them, and re-layouts  16.7 us (1%)
  between operations  15 us (1%)
  blocking collectives  11.7 us (1%)
    reduce_scatter x1, waiting for transfers between devices, local(): lax.psum_scatter(grad_up, 'fsdp', scatter_dimension=0, tiled=True)  121 us
    reduce_scatter x1, waiting for transfers between devices, local(): lax.psum_scatter(grad_down, 'fsdp', scatter_dimension=1, tiled=True)  120 us
    reduce_scatter x1, waiting for transfers between devices, local(): lax.psum_scatter(norm_part.reshape(seq_count, length, width), 'tp', scatt...  112 us
    reduce_scatter x1, waiting for transfers between devices, local(): lax.psum_scatter(grad_qkv, 'fsdp', scatter_dimension=0, tiled=True)  96.9 us
    reduce_scatter x1, waiting for transfers between devices, local(): lax.psum_scatter(branch_part.reshape(seq_count, length, width), 'tp', sca...  91.7 us
    all_gather x1, waiting for transfers between devices, local(): lax.all_gather(cotangent, 'tp', axis=1, tiled=True)  82.4 us
    all_gather x1, waiting for transfers between devices, local(): gathered = lax.all_gather(norm_output, 'tp', axis=1, tiled=True)  75.4 us
    all_gather x1, waiting for transfers between devices, local(): lax.all_gather(w_qkv, 'fsdp', axis=0, tiled=True)  47.5 us
  transfers between devices with their start and end apart: 13, of which 12 were waited for; matrix products, arithmetic and copies ran while one was open for 17% of the time, Pallas kernels for 0%

commit v1 on v0

v1 whole, which is shorter than its diff:
```python
import functools

import jax
import jax.numpy as jnp
from jax import lax
from jax.experimental import pallas as pl
from jax.experimental.pallas import tpu as pltpu
from jax.sharding import PartitionSpec as P

HEADS = 32
HEAD_DIM = 64
ROT = 32
PAIR = 2 * HEAD_DIM
BF = jnp.bfloat16
F32 = jnp.float32
VMEM_BYTES = 56 * 1024 * 1024

NN = (((1,), (0,)), ((), ()))
NT = (((1,), (1,)), ((), ()))
TN = (((0,), (0,)), ((), ()))


def dot(a, b, dims):
    return lax.dot_general(a, b, dims, preferred_element_type=F32)


def params():
    return pltpu.CompilerParams(vmem_limit_bytes=VMEM_BYTES)


def cost(flops, arrays, shapes, transcendentals=0):
    moved = sum(a.size * a.dtype.itemsize for a in list(arrays) + list(shapes))
    return pl.CostEstimate(flops=flops, bytes_accessed=moved, transcendentals=transcendentals)


def angle_tables(length):
    half_rot = ROT // 2
    position = jnp.arange(length, dtype=jnp.int32).astype(F32)[:, None]
    channel = jnp.arange(PAIR, dtype=jnp.int32) % HEAD_DIM
    exponent = (2 * (channel % half_rot)).astype(F32) / ROT
    angles = position * (10000.0 ** (-exponent))[None, :]
    low = (channel < half_rot)[None, :]
    inside = (channel < ROT)[None, :]
    cosine = jnp.where(inside, jnp.cos(angles), 1.0)
    sine = jnp.sin(angles)
    return (
        cosine,
        jnp.where(inside & ~low, sine, 0.0),
        jnp.where(low, -sine, 0.0),
    )


def turn(z, c, a, b):
    return z * c + pltpu.roll(z, ROT // 2, 1) * a + pltpu.roll(z, PAIR - ROT // 2, 1) * b


def turn_back(z, c, a, b):
    return z * c - pltpu.roll(z, ROT // 2, 1) * a - pltpu.roll(z, PAIR - ROT // 2, 1) * b


def attend_forward_kernel(block, q_in, k_in, v_in, c_ref, a_ref, b_ref, q_ref, k_ref, v_ref, o_ref, lse_ref):
    length = q_in.shape[0]
    c, a, b = c_ref[...], a_ref[...], b_ref[...]
    q = (turn(q_in[...], c, a, b) * HEAD_DIM**-0.5).astype(BF)
    k = turn(k_in[...], c, a, b).astype(BF)
    v = v_in[...].astype(BF)
    q_ref[...] = q
    k_ref[...] = k
    v_ref[...] = v
    q_t = q.T
    v_t = v.T
    head_row = lax.broadcasted_iota(jnp.int32, (PAIR, 1), 0) // HEAD_DIM
    key_at = lax.broadcasted_iota(jnp.int32, (block, block), 0)
    query_at = lax.broadcasted_iota(jnp.int32, (block, block), 1)
    allowed = key_at <= query_at
    for j in range(length // block):
        cols = slice(j * block, (j + 1) * block)
        done = j * block
        outs = []
        for h in range(2):
            q_h = jnp.where(head_row == h, q_t[:, cols], jnp.zeros((), BF))
            s_diag = jnp.where(allowed, dot(k[cols], q_h, NN), -1e30)
            largest = jnp.max(s_diag, axis=0, keepdims=True)
            if j:
                s_past = dot(k[:done], q_h, NN)
                largest = jnp.maximum(largest, jnp.max(s_past, axis=0, keepdims=True))
            p_diag = jnp.exp(s_diag - largest)
            total = jnp.sum(p_diag, axis=0, keepdims=True)
            rows = slice(h * HEAD_DIM, (h + 1) * HEAD_DIM)
            out = dot(v_t[rows, cols], p_diag.astype(BF), NN)
            if j:
                p_past = jnp.exp(s_past - largest)
                total = total + jnp.sum(p_past, axis=0, keepdims=True)
                out = out + dot(v_t[rows, :done], p_past.astype(BF), NN)
            outs.append(out / total)
            lse_ref[0, h : h + 1, cols] = largest + jnp.log(total)
        o_ref[cols, :] = jnp.concatenate(outs, axis=0).T.astype(BF)


def attend_forward(qkv, tables, heads_here):
    length = qkv.shape[0]
    pairs = heads_here // 2
    width = heads_here * HEAD_DIM
    block = min(256, length)

    def part(n):
        return pl.BlockSpec((length, PAIR), lambda p: (0, n * pairs + p))

    head = pl.BlockSpec((length, PAIR), lambda p: (0, p))
    table = pl.BlockSpec((length, PAIR), lambda p: (0, 0))
    shapes = [jax.ShapeDtypeStruct((length, width), BF)] * 4 + [
        jax.ShapeDtypeStruct((pairs, 8, length), F32)
    ]
    return pl.pallas_call(
        functools.partial(attend_forward_kernel, block),
        grid=(pairs,),
        in_specs=[part(0), part(1), part(2), table, table, table],
        out_specs=[head] * 4 + [pl.BlockSpec((1, 8, length), lambda p: (p, 0, 0))],
        out_shape=shapes,
        compiler_params=params(),
        cost_estimate=cost(16 * length * length * width, [qkv, *tables], shapes, length * length * heads_here // 2),
        name="attend_forward",
    )(qkv, qkv, qkv, *tables)


def attend_backward_kernel(block, q_ref, k_ref, v_ref, g_ref, lse_ref, c_ref, a_ref, b_ref, dq_ref, dk_ref, dv_ref, dk_acc, dv_acc):
    length = q_ref.shape[0]
    q, k, v, g = q_ref[...], k_ref[...], v_ref[...], g_ref[...]
    q_t, g_t, k_t = q.T, g.T, k.T
    head_row = lax.broadcasted_iota(jnp.int32, (PAIR, 1), 0) // HEAD_DIM
    head_col = lax.broadcasted_iota(jnp.int32, (1, PAIR), 1) // HEAD_DIM
    key_at = lax.broadcasted_iota(jnp.int32, (block, block), 0)
    query_at = lax.broadcasted_iota(jnp.int32, (block, block), 1)
    allowed = key_at <= query_at
    dk_acc[...] = jnp.zeros_like(dk_acc)
    dv_acc[...] = jnp.zeros_like(dv_acc)
    zero = jnp.zeros((), BF)
    c, a, b = c_ref[...], a_ref[...], b_ref[...]
    for j in range(length // block):
        cols = slice(j * block, (j + 1) * block)
        done = j * block
        stop = done + block
        dq_rows = []
        for h in range(2):
            rows = slice(h * HEAD_DIM, (h + 1) * HEAD_DIM)
            q_th = jnp.where(head_row == h, q_t[:, cols], zero)
            g_th = jnp.where(head_row == h, g_t[:, cols], zero)
            q_h = jnp.where(head_col == h, q[cols], zero)
            g_h = jnp.where(head_col == h, g[cols], zero)
            lse = lse_ref[0, h : h + 1, cols]
            p_diag = jnp.where(allowed, jnp.exp(dot(k[cols], q_th, NN) - lse), 0.0)
            dp_diag = dot(v[cols], g_th, NN)
            pd_diag = p_diag * dp_diag
            delta = jnp.sum(pd_diag, axis=0, keepdims=True)
            if j:
                p_past = jnp.exp(dot(k[:done], q_th, NN) - lse)
                pd_past = p_past * dot(v[:done], g_th, NN)
                delta = delta + jnp.sum(pd_past, axis=0, keepdims=True)
            ds_diag = (pd_diag - p_diag * delta).astype(BF)
            dq = dot(k_t[rows, cols], ds_diag, NN)
            dk_acc[cols, :] += dot(ds_diag, q_h, NN)
            dv_acc[cols, :] += dot(p_diag.astype(BF), g_h, NN)
            if j:
                ds_past = (pd_past - p_past * delta).astype(BF)
                dq = dq + dot(k_t[rows, :done], ds_past, NN)
                dk_acc[:done, :] += dot(ds_past, q_h, NN)
                dv_acc[:done, :] += dot(p_past.astype(BF), g_h, NN)
            dq_rows.append(dq)
        dq_block = jnp.concatenate(dq_rows, axis=0).T * HEAD_DIM**-0.5
        dq_ref[cols, :] = turn_back(dq_block, c[cols], a[cols], b[cols]).astype(BF)
    dk_ref[...] = turn_back(dk_acc[...], c, a, b).astype(BF)
    dv_ref[...] = dv_acc[...].astype(BF)


def attend_backward(q, k, v, g, lse, tables):
    length, width = q.shape
    pairs = width // PAIR
    block = min(256, length)
    head = pl.BlockSpec((length, PAIR), lambda p: (0, p))
    table = pl.BlockSpec((length, PAIR), lambda p: (0, 0))
    shapes = [jax.ShapeDtypeStruct((length, width), BF)] * 3
    return pl.pallas_call(
        functools.partial(attend_backward_kernel, block),
        grid=(pairs,),
        in_specs=[head] * 4 + [pl.BlockSpec((1, 8, length), lambda p: (p, 0, 0)), table, table, table],
        out_specs=[head] * 3,
        out_shape=shapes,
        scratch_shapes=[pltpu.VMEM((length, PAIR), F32)] * 2,
        compiler_params=params(),
        cost_estimate=cost(40 * length * length * width, [q, k, v, g, *tables], shapes, length * length * pairs),
        name="attend_backward",
    )(q, k, v, g, lse, *tables)


def column_tiles(body, whole, tiled, extras, out_types, rows, columns, tile, flops, name, transcendentals=0):
    def spec(array, axis):
        if axis == 0:
            return pl.BlockSpec((tile, array.shape[1]), lambda j: (j, 0))
        return pl.BlockSpec((array.shape[0], tile), lambda j: (0, j))

    shapes = [jax.ShapeDtypeStruct((rows, columns), t) for t in out_types]
    arrays = [*whole, *[a for a, _ in tiled], *extras]
    return pl.pallas_call(
        body,
        grid=(columns // tile,),
        in_specs=[pl.BlockSpec(a.shape, lambda j: (0, 0), pipeline_mode=pl.Buffered(1)) for a in whole]
        + [spec(a, axis) for a, axis in tiled]
        + [pl.BlockSpec((rows, tile), lambda j: (0, j)) for _ in extras],
        out_specs=[pl.BlockSpec((rows, tile), lambda j: (0, j))] * len(shapes),
        out_shape=shapes,
        compiler_params=params(),
        cost_estimate=cost(flops, arrays, shapes, transcendentals),
        name=name,
    )(*arrays)


def project_kernel(x_ref, w_ref, out_ref):
    out_ref[...] = dot(x_ref[...], w_ref[...], NN).astype(out_ref.dtype)


def project(x, w, out_type, name):
    rows, depth = x.shape
    columns = w.shape[1]
    (out,) = column_tiles(
        project_kernel, [x], [(w, 1)], [], [out_type], rows, columns, min(256, columns), 2 * rows * depth * columns, name
    )
    return out


def project_back_kernel(x_ref, w_ref, out_ref):
    out_ref[...] = dot(x_ref[...], w_ref[...], NT).astype(out_ref.dtype)


def project_back(x, w, out_type, name):
    rows, depth = x.shape
    columns = w.shape[0]
    (out,) = column_tiles(
        project_back_kernel, [x], [(w, 0)], [], [out_type], rows, columns, min(256, columns), 2 * rows * depth * columns, name
    )
    return out


GELU_C = 0.7978845608028654
GELU_A = 0.044715


def up_kernel(x_ref, w_ref, hidden_ref, slope_ref):
    u = dot(x_ref[...], w_ref[...], NN)
    square = u * u
    t = jnp.tanh(GELU_C * (u + GELU_A * square * u))
    half = 0.5 * (1.0 + t)
    hidden_ref[...] = (u * half).astype(BF)
    slope_ref[...] = (half + 0.5 * u * (1.0 - t * t) * (GELU_C * (1.0 + 3.0 * GELU_A * square))).astype(BF)


def up_project(x, w):
    rows, depth = x.shape
    columns = w.shape[1]
    return column_tiles(
        up_kernel, [x], [(w, 1)], [], [BF, BF], rows, columns, min(256, columns), 2 * rows * depth * columns, "up", rows * columns
    )


def d_up_kernel(g_ref, w_ref, slope_ref, out_ref):
    out_ref[...] = (dot(g_ref[...], w_ref[...], NT) * slope_ref[...].astype(F32)).astype(BF)


def d_up_project(g, w, slope):
    rows, depth = g.shape
    columns = w.shape[0]
    (out,) = column_tiles(
        d_up_kernel, [g], [(w, 0)], [slope], [BF], rows, columns, min(256, columns), 2 * rows * depth * columns, "d_up"
    )
    return out


def branch_kernel(att_ref, hidden_ref, wo_ref, wd_ref, out_ref):
    out_ref[...] = (dot(att_ref[...], wo_ref[...], NN) + dot(hidden_ref[...], wd_ref[...], NN)).astype(BF)


def branch_project(att, hidden, w_out, w_down):
    rows = att.shape[0]
    columns = w_out.shape[1]
    (out,) = column_tiles(
        branch_kernel, [att, hidden], [(w_out, 1), (w_down, 1)], [], [BF], rows, columns, min(256, columns),
        2 * rows * columns * (att.shape[1] + hidden.shape[1]), "branch",
    )
    return out


def d_normed_kernel(dq_ref, dk_ref, dv_ref, du_ref, wq_ref, wu_ref, out_ref):
    part = dq_ref.shape[1]
    total = dot(du_ref[...], wu_ref[...], NT)
    for n, ref in enumerate((dq_ref, dk_ref, dv_ref)):
        total = total + dot(ref[...], wq_ref[:, n * part : (n + 1) * part], NT)
    out_ref[...] = total.astype(BF)


def d_normed_project(dqkv, d_up, w_qkv, w_up):
    rows = d_up.shape[0]
    columns = w_up.shape[0]
    (out,) = column_tiles(
        d_normed_kernel, [*dqkv, d_up], [(w_qkv, 0), (w_up, 0)], [], [BF], rows, columns, min(256, columns),
        2 * rows * columns * (w_qkv.shape[1] + w_up.shape[1]), "d_normed",
    )
    return out


def weight_grad_kernel(count, with_sum, *refs):
    x_ref, rights, rest = refs[0], refs[1 : 1 + count], refs[1 + count :]
    out_ref = rest[-1]
    x_t = x_ref[...].T
    start = 0
    for right in rights:
        stop = start + right.shape[1]
        total = dot(x_t, right[...], NN)
        if with_sum:
            total = total + rest[0][:, start:stop].astype(F32)
        out_ref[:, start:stop] = total.astype(BF)
        start = stop


def weight_grad(x, rights, half, arrived, name):
    tokens, width = x.shape
    rows = width // 2
    columns = sum(r.shape[1] for r in rights)
    tile = min(256, rows)
    first = half * (rows // tile)
    out = pl.BlockSpec((tile, columns), lambda j: (j, 0))
    shape = jax.ShapeDtypeStruct((rows, columns), BF)
    extras = [] if arrived is None else [arrived]
    return pl.pallas_call(
        functools.partial(weight_grad_kernel, len(rights), bool(extras)),
        grid=(rows // tile,),
        in_specs=[pl.BlockSpec((tokens, tile), lambda j: (0, first + j))]
        + [pl.BlockSpec(r.shape, lambda j: (0, 0), pipeline_mode=pl.Buffered(1)) for r in rights]
        + [out for _ in extras],
        out_specs=out,
        out_shape=shape,
        compiler_params=params(),
        cost_estimate=cost(2 * tokens * rows * columns, [x, *rights, *extras], [shape]),
        name=name,
    )(x, *rights, *extras)


def flip(array, bit):
    count = lax.axis_size("fsdp")
    return lax.ppermute(array, "fsdp", [(s, s ^ bit) for s in range(count)])


def chip_bits():
    bits, bit = [], 2
    while bit < lax.axis_size("fsdp"):
        bits.append(bit)
        bit *= 2
    return bits


def split(array, axis):
    size = array.shape[axis] // 2
    return lax.slice_in_dim(array, 0, size, axis=axis), lax.slice_in_dim(array, size, 2 * size, axis=axis)


def gather_weight(own, axis):
    bits = chip_bits()
    got = {0: own}
    if len(bits) == 2:
        x, y = bits
        got[x], got[y] = flip(own, x), flip(own, y)
        first, second = split(got[y], axis)[0], split(got[x], axis)[1]
        got[x | y] = jnp.concatenate([flip(first, x), flip(second, y)], axis=axis)
    else:
        for bit in bits:
            for r in list(got):
                got[r | bit] = flip(got[r], bit)
    mine = jnp.concatenate([got[r] for r in sorted(got)], axis=axis)
    return jnp.concatenate([mine, flip(mine, 1)], axis=axis)


def scatter_grad(parts):
    bits = chip_bits()
    held = {2 * p: part for p, part in enumerate(parts)}

    def add(a, b):
        return a.astype(F32) + b.astype(F32)

    if len(bits) == 2:
        x, y = bits
        first, second = split(held[x | y], 0)
        via_x, via_y = flip(first, x), flip(second, y)
        size = first.shape[0]
        to_y = jnp.concatenate([add(held[y][:size], via_x).astype(BF), held[y][size:]], axis=0)
        to_x = jnp.concatenate([held[x][:size], add(held[x][size:], via_y).astype(BF)], axis=0)
        return add(held[0], flip(to_x, x)) + flip(to_y, y).astype(F32)
    for bit in reversed(bits):
        for r in [r for r in held if not r & bit]:
            total = add(held[r], flip(held.pop(r | bit), bit))
            held[r] = total if bit == bits[0] else total.astype(BF)
    return held[0]


def reduce_weight_grad(x, rights, name):
    chips = lax.axis_size("fsdp") // 2
    away = weight_grad(x, rights, 1, None, name + "_away")
    mine = weight_grad(x, rights, 0, flip(away, 1), name + "_mine")
    size = mine.shape[0] // chips
    return scatter_grad([mine[p * size : (p + 1) * size] for p in range(chips)])


def place_order():
    count = lax.axis_size("fsdp")
    return list(range(0, count, 2)) + list(range(1, count, 2))


def to_relative(array):
    order = place_order()
    me = lax.axis_index("fsdp")
    size = array.shape[-1] // len(order)
    return jnp.concatenate(
        [lax.dynamic_slice_in_dim(array, (me ^ r) * size, size, axis=-1) for r in order], axis=-1
    )


def to_absolute(array):
    order = place_order()
    me = lax.axis_index("fsdp")
    size = array.shape[-1] // len(order)
    places = jnp.array([order.index(r) for r in range(len(order))], jnp.int32)
    return jnp.concatenate(
        [lax.dynamic_slice_in_dim(array, places[me ^ b] * size, size, axis=-1) for b in range(len(order))], axis=-1
    )


def line_gather(block):
    n = lax.axis_size("tp")
    me = lax.axis_index("tp")
    up, down = {}, {}
    moving_up = moving_down = block
    for s in range(1, n):
        up[s] = moving_up = lax.ppermute(moving_up, "tp", [(i, i + 1) for i in range(s - 1, n - 1)])
        down[s] = moving_down = lax.ppermute(moving_down, "tp", [(i, i - 1) for i in range(1, n - s + 1)])
    rows = block.shape[0]
    out = jnp.zeros((n * rows, block.shape[1]), block.dtype)
    out = lax.dynamic_update_slice_in_dim(out, block, me * rows, axis=0)
    for d in range(1, n):
        piece = jnp.where(me >= d, up[d], down[n - d])
        out = lax.dynamic_update_slice_in_dim(out, piece, lax.rem(me - d + n, n) * rows, axis=0)
    return out


def line_scatter(part):
    n = lax.axis_size("tp")
    me = lax.axis_index("tp")
    rows = part.shape[0] // n

    def take(j):
        return lax.dynamic_slice_in_dim(part, lax.rem(j, n) * rows, rows, axis=0)

    up = down = None
    for s in range(1, n):
        out_up, out_down = take(me + n - s), take(me + s)
        if s > 1:
            out_up = (out_up.astype(F32) + up.astype(F32)).astype(BF)
            out_down = (out_down.astype(F32) + down.astype(F32)).astype(BF)
        up = lax.ppermute(out_up, "tp", [(i, i + 1) for i in range(s)])
        down = lax.ppermute(out_down, "tp", [(i, i - 1) for i in range(n - 1, n - 1 - s, -1)])
    total = take(me).astype(F32)
    if up is not None:
        total = total + up.astype(F32) + down.astype(F32)
    return total


def local(tokens, gain, bias, w_qkv, w_out, w_up, w_down, cotangent):
    _, own_rows, width = tokens.shape
    groups = lax.axis_size("tp")
    heads_here = HEADS // groups
    part = heads_here * HEAD_DIM
    length = own_rows * groups
    tokens_f = tokens[0].astype(F32)
    average = jnp.mean(tokens_f, axis=-1, keepdims=True)
    centered = tokens_f - average
    inverse = lax.rsqrt(jnp.mean(centered * centered, axis=-1, keepdims=True) + 1e-05)
    xhat = centered * inverse
    normed_own = to_relative((xhat * gain + bias).astype(BF))
    cot_own = to_relative(cotangent[0])

    normed = line_gather(normed_own)
    cot = line_gather(cot_own)
    full_up = gather_weight(w_up, 0)
    full_qkv = gather_weight(w_qkv.reshape(w_qkv.shape[0], 3 * part), 0)
    full_down = gather_weight(w_down, 1)
    full_out = gather_weight(w_out, 1)

    tables = angle_tables(length)
    qkv = project(normed, full_qkv, F32, "qkv")
    q, k, v, attended, lse = attend_forward(qkv, tables, heads_here)
    hidden, slope = up_project(normed, full_up)
    branch = branch_project(attended, hidden, full_out, full_down)
    summed = to_absolute(line_scatter(branch))
    output = (tokens_f + summed).astype(BF)[None]

    grad_down = reduce_weight_grad(cot, [hidden], "down_grad")
    d_up = d_up_project(cot, full_down, slope)
    grad_up = reduce_weight_grad(normed, [d_up], "up_grad")
    d_att = project_back(cot, full_out, BF, "d_att")
    grad_out = reduce_weight_grad(cot, [attended], "out_grad")
    dqkv = attend_backward(q, k, v, d_att, lse, tables)
    d_normed_part = d_normed_project(dqkv, d_up, full_qkv, full_up)
    grad_qkv = reduce_weight_grad(normed, list(dqkv), "qkv_grad")

    d_normed = to_absolute(line_scatter(d_normed_part))
    stats = jnp.stack([jnp.sum(d_normed * xhat, axis=0), jnp.sum(d_normed, axis=0)], axis=0)
    stats = lax.psum(stats, ("fsdp", "tp"))
    own_width = width // lax.axis_size("fsdp")
    stats = lax.dynamic_slice_in_dim(stats, lax.axis_index("fsdp") * own_width, own_width, axis=1)
    d_hat = d_normed * gain
    in_grad = cotangent[0].astype(F32) + inverse * (
        d_hat
        - jnp.mean(d_hat, axis=-1, keepdims=True)
        - xhat * jnp.mean(d_hat * xhat, axis=-1, keepdims=True)
    )
    return (
        output,
        in_grad[None],
        stats[0],
        stats[1],
        grad_qkv.reshape(grad_qkv.shape[0], 3, part),
        grad_out.T,
        grad_up,
        grad_down.T,
    )


def solution(mesh):
    return jax.shard_map(
        local,
        mesh=mesh,
        in_specs=(
            P("fsdp", "tp", None),
            P(),
            P(),
            P("fsdp", None, "tp"),
            P("tp", "fsdp"),
            P("fsdp", "tp"),
            P("tp", "fsdp"),
            P("fsdp", "tp", None),
        ),
        out_specs=(
            P("fsdp", "tp", None),
            P("fsdp", "tp", None),
            P("fsdp"),
            P("fsdp"),
            P("fsdp", None, "tp"),
            P("tp", "fsdp"),
            P("fsdp", "tp"),
            P("tp", "fsdp"),
        ),
        check_vma=False,
    )
```

time: 1140 us -> 712 us (0.62)
  waiting for transfers between devices: 867 us -> 160 us
  Pallas kernels: 0 us -> 191 us
  matrix products: 181 us -> 0 us
  starting transfers between devices: 0.53 us -> 144 us
  local copies, waits for them, and re-layouts: 16.7 us -> 88.7 us
  blocking collectives: 11.7 us -> 55.7 us
  other arithmetic: 44.3 us -> 55.7 us
    reduce_scatter x6 -> x0, waiting for transfers between devices: 583 us -> none  [the longest x1 121 us: local(): lax.psum_scatter(grad_up, 'fsdp', scatter_dimension=0, tiled=True)]
    all_gather x6 -> x0, waiting for transfers between devices: 246 us -> none  [the longest x1 82.4 us: local(): lax.all_gather(cotangent, 'tp', axis=1, tiled=True)]
    pallas_call x0 -> x16, Pallas kernels: none -> 191 us  [the longest x6 88.3 us: column_tiles(): pl.pallas_call(body, grid=(columns // tile,), in_specs=[pl.BlockSpec(a.sh...]
    dot_general x24 -> x0, matrix products: 181 us -> none  [the longest x1 18.3 us: local(): jnp.einsum('td,fd->tf', cot_rows, full_down, preferred_element_type=jnp.f...]
    ppermute x0 -> x64, waiting for transfers between devices: none -> 160 us  [the longest x6 62.6 us: line_gather(): lax.ppermute(moving_down, 'tp', [(i, i - 1) for i in range(1, n - s + 1)])]
    ppermute x0 -> x64, starting transfers between devices: none -> 144 us  [the longest x6 86.1 us: line_scatter(): up = lax.ppermute(out_up, 'tp', [(i, i + 1) for i in range(s)])]
    psum x1, blocking collectives: 11.7 us -> 55.7 us  [local(): stats = lax.psum(stats, ('fsdp', 'tp'))]
    unnamed x14 -> x0, waiting for transfers between devices: 38 us -> none
  transfers between devices with their start and end apart: 13 -> 64, of which waited for: 12 -> 17; matrix products, arithmetic and copies ran while one was open for 17% -> 20% of each run, Pallas kernels for 0% -> 27%
where the time goes in v1:
time: 712 us; the launch traced here: 701 us
  Pallas kernels  191 us (27%)
  waiting for transfers between devices  160 us (22%)
  starting transfers between devices  144 us (20%)
  local copies, waits for them, and re-layouts  88.7 us (12%)
  other arithmetic  55.7 us (8%)
  blocking collectives  55.7 us (8%)
    pallas_call x6, Pallas kernels, column_tiles(): pl.pallas_call(body, grid=(columns // tile,), in_specs=[pl.BlockSpec(a.sh...  88.3 us
    ppermute x6, starting transfers between devices, line_scatter(): up = lax.ppermute(out_up, 'tp', [(i, i + 1) for i in range(s)])  86.1 us
    ppermute x6, waiting for transfers between devices, line_gather(): lax.ppermute(moving_down, 'tp', [(i, i - 1) for i in range(1, n - s + 1)])  62.6 us
    pallas_call x8, Pallas kernels, weight_grad(): pl.pallas_call(functools.partial(weight_grad_kernel, len(rights), bool(ex...  62.3 us
    ppermute x40, waiting for transfers between devices, flip(): return lax.ppermute(array, 'fsdp', [(s, s ^ bit) for s in range(count)])  59.6 us
    psum x1, blocking collectives, local(): stats = lax.psum(stats, ('fsdp', 'tp'))  55.7 us
    unnamed x96, local copies, waits for them, and re-layouts  47.2 us
    ppermute x40, starting transfers between devices, flip(): return lax.ppermute(array, 'fsdp', [(s, s ^ bit) for s in range(count)])  31.4 us
  transfers between devices with their start and end apart: 64, of which 17 were waited for; matrix products, arithmetic and copies ran while one was open for 20% of the time, Pallas kernels for 27%

profile of v1, /device:TPU:0, one launch (start us, length us, event | category | flops | bytes accessed | tf_op | source)
XLA Modules:
  0.0 701.3 jit_solution(10262629117745264060)
XLA Ops:
  0.7 3.0 collective-permute-start.16
  14.4 4.5 collective-permute-start
  28.2 2.9 constant_dynamic-update-slice_fusion.23
  31.1 2.6 broadcast.203.clone
  36.0 3.2 fusion.23
  54.0 10.3 %collective-permute-done.18 = bf16[512,128]{1,0:T(8,128)(2,1)S(1)} collective-permute-done((bf16[512,128]{1,0:T(8,128)(2,1)S(1)}, bf16[512,128]{1,0:T(8,128)(2,1)S(1)}, u32[]{:S(2)}, u32[]{:S(2)}) %collective-permute-start.18) | collective-permute-done | bytes 131104 | tf_op jit(solution)/shard_map/ppermute | solution.py:348
  65.9 3.6 collective-permute-done.19
  83.4 12.5 %collective-permute-done.22 = bf16[2048,256]{1,0:T(8,128)(2,1)S(1)} collective-permute-done((bf16[2048,256]{1,0:T(8,128)(2,1)}, bf16[2048,256]{1,0:T(8,128)(2,1)S(1)}, u32[]{:S(2)}, u32[]{:S(2)}) %collective-permute-start.22) | collective-permute-done | bytes 1048608 | tf_op jit(solution)/shard_map/ppermute | solution.py:348
  98.5 2.6 collective-permute-start.32
  101.0 15.3 %collective-permute-done.33 = bf16[256,2048]{1,0:T(8,128)(2,1)S(1)} collective-permute-done((bf16[256,2048]{1,0:T(8,128)(2,1)}, bf16[256,2048]{1,0:T(8,128)(2,1)S(1)}, u32[]{:S(2)}, u32[]{:S(2)}) %collective-permute-start.33) | collective-permute-done | bytes 1048608 | tf_op jit(solution)/shard_map/ppermute | solution.py:441
  123.1 4.7 collective-permute-done.9
  133.1 2.5 collective-permute-done.23
  136.3 9.4 %collective-permute-done.34 = bf16[256,2048]{1,0:T(8,128)(2,1)S(1)} collective-permute-done((bf16[256,2048]{1,0:T(8,128)(2,1)S(1)}, bf16[256,2048]{1,0:T(8,128)(2,1)S(1)}, u32[]{:S(2)}, u32[]{:S(2)}) %collective-permute-start.34) | collective-permute-done | bytes 1048608 | tf_op jit(solution)/shard_map/ppermute | solution.py:441
  151.7 7.9 %collective-permute-done.14 = bf16[128,2048]{1,0:T(8,128)(2,1)S(1)} collective-permute-done((bf16[128,2048]{1,0:T(8,128)(2,1)S(1)}, bf16[128,2048]{1,0:T(8,128)(2,1)S(1)}, u32[]{:S(2)}, u32[]{:S(2)}) %collective-permute-start.14) | collective-permute-done | bytes 524320 | tf_op jit(solution)/shard_map/ppermute | solution.py:348
  160.8 7.3 %collective-permute-done.2 = bf16[256,2048]{1,0:T(8,128)(2,1)S(1)} collective-permute-done((bf16[256,2048]{1,0:T(8,128)(2,1)S(1)}, bf16[256,2048]{1,0:T(8,128)(2,1)S(1)}, u32[]{:S(2)}, u32[]{:S(2)}) %collective-permute-start.2) | collective-permute-done | bytes 1048608 | tf_op jit(solution)/shard_map/ppermute | solution.py:441
  169.4 21.2 %collective-permute-done.35 = bf16[256,2048]{1,0:T(8,128)(2,1)S(1)} collective-permute-done((bf16[256,2048]{1,0:T(8,128)(2,1)S(1)}, bf16[256,2048]{1,0:T(8,128)(2,1)S(1)}, u32[]{:S(2)}, u32[]{:S(2)}) %collective-permute-start.35) | collective-permute-done | bytes 1048608 | tf_op jit(solution)/shard_map/ppermute | solution.py:441
  197.2 6.4 d_att.1.g_ref
  203.5 9.0 %collective-permute-done.3 = bf16[256,2048]{1,0:T(8,128)(2,1)} collective-permute-done((bf16[256,2048]{1,0:T(8,128)(2,1)S(1)}, bf16[256,2048]{1,0:T(8,128)(2,1)}, u32[]{:S(2)}, u32[]{:S(2)}) %collective-permute-start.3) | collective-permute-done | bytes 1048608 | tf_op jit(solution)/shard_map/ppermute | solution.py:441
  212.5 2.6 select_dynamic-update-slice_fusion.5
  217.9 3.7 constant_dynamic-update-slice_fusion.13.w_ref.wq_ref
  221.6 11.9 %qkv.1.q_in.k_in.v_in = f32[1024,1536]{1,0:T(8,128)} custom-call(bf16[1024,2048]{1,0:T(8,128)(2,1)} %select_dynamic-update-slice_fusion.3.x_ref.refs_0_, bf16[2048,1536]{1,0:T(8,128)(2,1)} %constant_dynamic-update-slice_fusion.13.w_ref.wq_ref), custom_call_target="tpu_custom_call" | custom-call | flops 6442450944 | bytes 16777216 | tf_op jit(solution)/shard_map/qkv/pallas_call | solution.py:203
  233.6 16.9 %attend_forward.1 = (bf16[1024,512]{1,0:T(8,128)(2,1)}, bf16[1024,512]{1,0:T(8,128)(2,1)}, bf16[1024,512]{1,0:T(8,128)(2,1)}, bf16[1024,512]{1,0:T(8,128)(2,1)}, f32[4,8,1024]{2,1,0:T(8,128)}) custom-call(f32[1024,1536]{1,0:T(8,128)} %qkv.1.q_in.k_in.v_in, f32[1024,1536]{1,0:T(8,128)} %qkv.1.q_in.k_in.v_in, f32[1024,1536]{1,0:T(8,128)} %qkv.1.q_in.k_in.v_in, ...), custom_call_target="tpu_custom_call" | custom-call | flops 8589934592 | bytes 12189696 | tf_op jit(solution)/shard_map/attend_forward/pallas_call | solution.py:114
  250.5 4.8 out_grad_away.1
  255.3 23.2 %attend_backward.1 = (bf16[1024,512]{1,0:T(8,128)(2,1)}, bf16[1024,512]{1,0:T(8,128)(2,1)}, bf16[1024,512]{1,0:T(8,128)(2,1)}) custom-call(bf16[1024,512]{1,0:T(8,128)(2,1)} %get-tuple-element.20.q_ref, bf16[1024,512]{1,0:T(8,128)(2,1)} %get-tuple-element.21.k_ref, bf16[1024,512]{1,0:T(8,128)(2,1)} %get-tuple-element.22.v_ref, ...), custom_call_target="tpu_custom_call" | custom-call | flops 21474836480 | bytes 8912896 | tf_op jit(solution)/shard_map/attend_backward/pallas_call | solution.py:182
  279.6 5.2 out_grad_mine.1
  287.0 7.6 %qkv_grad_away.1 = bf16[1024,1536]{1,0:T(8,128)(2,1)} custom-call(bf16[1024,2048]{1,0:T(8,128)(2,1)} %select_dynamic-update-slice_fusion.3.x_ref.refs_0_, bf16[1024,512]{1,0:T(8,128)(2,1)} %get-tuple-element.24.dq_ref.refs_1_, bf16[1024,512]{1,0:T(8,128)(2,1)} %get-tuple-element.25.dk_ref.refs_2_, bf16[1024,512]{1,0:T(8,128)(2,1)} %get-tuple-element.26.dv_ref.refs_3_), custom_call_target="tpu_custom_call" | custom-call | flops 3221225472 | bytes 10485760 | tf_op jit(solution)/shard_map/qkv_grad_away/pallas_call | solution.py:332
  298.5 4.8 constant_dynamic-update-slice_fusion.24.w_ref.wu_ref
  303.3 17.2 %up.1 = (bf16[1024,2048]{1,0:T(8,128)(2,1)}, bf16[1024,2048]{1,0:T(8,128)(2,1)}) custom-call(bf16[1024,2048]{1,0:T(8,128)(2,1)} %select_dynamic-update-slice_fusion.3.x_ref.refs_0_, bf16[2048,2048]{1,0:T(8,128)(2,1)} %constant_dynamic-update-slice_fusion.24.w_ref.wu_ref), custom_call_target="tpu_custom_call" | custom-call | flops 8589934592 | bytes 20971520 | tf_op jit(solution)/shard_map/up/pallas_call | solution.py:203
  322.9 15.2 %d_up.1.du_ref.refs_1_ = bf16[1024,2048]{1,0:T(8,128)(2,1)} custom-call(bf16[1024,2048]{1,0:T(8,128)(2,1)} %select_dynamic-update-slice_fusion.x_ref.g_ref.refs_0_, bf16[2048,2048]{1,0:T(8,128)(2,1)} %constant_dynamic-update-slice_fusion.46.wd_ref.w_ref, bf16[1024,2048]{1,0:T(8,128)(2,1)} %get-tuple-element.27.slope_ref), custom_call_target="tpu_custom_call" | custom-call | flops 8589934592 | bytes 20971520 | tf_op jit(solution)/shard_map/d_up/pallas_call | solution.py:203
  338.1 21.5 %d_normed.1 = bf16[1024,2048]{1,0:T(8,128)(2,1)} custom-call(bf16[1024,512]{1,0:T(8,128)(2,1)} %get-tuple-element.24.dq_ref.refs_1_, bf16[1024,512]{1,0:T(8,128)(2,1)} %get-tuple-element.25.dk_ref.refs_2_, bf16[1024,512]{1,0:T(8,128)(2,1)} %get-tuple-element.26.dv_ref.refs_3_, bf16[1024,2048]{1,0:T(8,128)(2,1)} %d_up.1.du_ref.refs_1_, ...), custom_call_target="tpu_custom_call" | custom-call | flops 15032385536 | bytes 26214400 | tf_op jit(solution)/shard_map/d_normed/pallas_call | solution.py:203
  363.3 16.1 %branch.1 = bf16[1024,2048]{1,0:T(8,128)(2,1)} custom-call(bf16[1024,512]{1,0:T(8,128)(2,1)} %get-tuple-element.18.att_ref.refs_1_, bf16[1024,2048]{1,0:T(8,128)(2,1)} %get-tuple-element.19.hidden_ref.refs_1_, bf16[512,2048]{1,0:T(8,128)(2,1)} %copy-done.14, bf16[2048,2048]{1,0:T(8,128)(2,1)} %constant_dynamic-update-slice_fusion.46.wd_ref.w_ref), custom_call_target="tpu_custom_call" | custom-call | flops 10737418240 | bytes 19922944 | tf_op jit(solution)/shard_map/branch/pallas_call | solution.py:203
  383.0 8.7 %up_grad_away.1 = bf16[1024,2048]{1,0:T(8,128)(2,1)} custom-call(bf16[1024,2048]{1,0:T(8,128)(2,1)} %select_dynamic-update-slice_fusion.3.x_ref.refs_0_, bf16[1024,2048]{1,0:T(8,128)(2,1)} %d_up.1.du_ref.refs_1_), custom_call_target="tpu_custom_call" | custom-call | flops 4294967296 | bytes 12582912 | tf_op jit(solution)/shard_map/up_grad_away/pallas_call | solution.py:332
  391.7 8.7 %down_grad_away.1 = bf16[1024,2048]{1,0:T(8,128)(2,1)} custom-call(bf16[1024,2048]{1,0:T(8,128)(2,1)} %select_dynamic-update-slice_fusion.x_ref.g_ref.refs_0_, bf16[1024,2048]{1,0:T(8,128)(2,1)} %get-tuple-element.19.hidden_ref.refs_1_), custom_call_target="tpu_custom_call" | custom-call | flops 4294967296 | bytes 12582912 | tf_op jit(solution)/shard_map/down_grad_away/pallas_call | solution.py:332
  402.0 2.9 fusion.2
  409.9 14.0 %collective-permute-start.27 = (bf16[256,2048]{1,0:T(8,128)(2,1)S(1)}, bf16[256,2048]{1,0:T(8,128)(2,1)S(1)}, u32[]{:S(2)}, u32[]{:S(2)}) collective-permute-start(bf16[256,2048]{1,0:T(8,128)(2,1)S(1)} %fusion), channel_id=1, source_target_pairs={{0,1},{1,2},{4,5},{5,6},{8,9},{9,10},{12,13},{13,14},{16,17},{17,1... | collective-permute-start | bytes 3145736 | tf_op jit(solution)/shard_map/ppermute | solution.py:465
  424.0 8.1 %qkv_grad_mine.1 = bf16[1024,1536]{1,0:T(8,128)(2,1)} custom-call(bf16[1024,2048]{1,0:T(8,128)(2,1)} %select_dynamic-update-slice_fusion.3.x_ref.refs_0_, bf16[1024,512]{1,0:T(8,128)(2,1)} %get-tuple-element.24.dq_ref.refs_1_, bf16[1024,512]{1,0:T(8,128)(2,1)} %get-tuple-element.25.dk_ref.refs_2_, bf16[1024,512]{1,0:T(8,128)(2,1)} %get-tuple-element.26.dv_ref.refs_3_, ...), custom_call_target="tpu_custom_call" | custom-call | flops 3221225472 | bytes 13631488 | tf_op jit(solution)/shard_map/qkv_grad_mine/pallas_call | solution.py:332
  436.0 16.4 %collective-permute-done.27 = bf16[256,2048]{1,0:T(8,128)(2,1)S(1)} collective-permute-done((bf16[256,2048]{1,0:T(8,128)(2,1)S(1)}, bf16[256,2048]{1,0:T(8,128)(2,1)S(1)}, u32[]{:S(2)}, u32[]{:S(2)}) %collective-permute-start.27) | collective-permute-done | bytes 1048608 | tf_op jit(solution)/shard_map/ppermute | solution.py:465
  461.5 13.5 %collective-permute-done.48 = bf16[256,1536]{1,0:T(8,128)(2,1)S(1)} collective-permute-done((bf16[256,1536]{1,0:T(8,128)(2,1)S(1)}, bf16[256,1536]{1,0:T(8,128)(2,1)S(1)}, u32[]{:S(2)}, u32[]{:S(2)}) %collective-permute-start.48) | collective-permute-done | bytes 786464 | tf_op jit(solution)/shard_map/ppermute | solution.py:348
  474.9 15.5 %collective-permute-start.40 = (bf16[256,2048]{1,0:T(8,128)(2,1)}, bf16[256,2048]{1,0:T(8,128)(2,1)}, u32[]{:S(2)}, u32[]{:S(2)}) collective-permute-start(bf16[256,2048]{1,0:T(8,128)(2,1)} %get-tuple-element.48), channel_id=1, source_target_pairs={{0,1},{1,2},{2,3},{4,5},{5,6},{6,7},{8,9},{9,10},{10,11},{12,13},{... | collective-permute-start | bytes 3145736 | tf_op jit(solution)/shard_map/ppermute | solution.py:465
  494.5 50.5 %collective-permute-start.28 = (bf16[256,2048]{1,0:T(8,128)(2,1)S(1)}, bf16[256,2048]{1,0:T(8,128)(2,1)S(1)}, u32[]{:S(2)}, u32[]{:S(2)}) collective-permute-start(bf16[256,2048]{1,0:T(8,128)(2,1)S(1)} %copy-done.9), channel_id=1, source_target_pairs={{0,1},{1,2},{2,3},{4,5},{5,6},{6,7},{8,9},{9,10},{10,11},{12,13},{... | collective-permute-start | bytes 3145736 | tf_op jit(solution)/shard_map/ppermute | solution.py:465
  550.2 9.7 %up_grad_mine.1 = bf16[1024,2048]{1,0:T(8,128)(2,1)} custom-call(bf16[1024,2048]{1,0:T(8,128)(2,1)} %select_dynamic-update-slice_fusion.3.x_ref.refs_0_, bf16[1024,2048]{1,0:T(8,128)(2,1)} %d_up.1.du_ref.refs_1_, bf16[1024,2048]{1,0:T(8,128)(2,1)} %collective-permute-done.54.refs_2_), custom_call_target="tpu_custom_call" | custom-call | flops 4294967296 | bytes 16777216 | tf_op jit(solution)/shard_map/up_grad_mine/pallas_call | solution.py:332
  559.9 2.6 fusion.32
  563.5 9.6 %down_grad_mine.1 = bf16[1024,2048]{1,0:T(8,128)(2,1)} custom-call(bf16[1024,2048]{1,0:T(8,128)(2,1)} %select_dynamic-update-slice_fusion.x_ref.g_ref.refs_0_, bf16[1024,2048]{1,0:T(8,128)(2,1)} %get-tuple-element.19.hidden_ref.refs_1_, bf16[1024,2048]{1,0:T(8,128)(2,1)} %collective-permute-done.59.refs_2_), custom_call_target="tpu_custom_call" | custom-call | flops 4294967296 | bytes 16777216 | tf_op jit(solution)/shard_map/down_grad_mine/pallas_call | solution.py:332
  581.6 4.5 collective-permute-done.60
  604.6 19.2 %collective-permute-done.31 = bf16[256,2048]{1,0:T(8,128)(2,1)S(1)} collective-permute-done((bf16[256,2048]{1,0:T(8,128)(2,1)S(1)}, bf16[256,2048]{1,0:T(8,128)(2,1)S(1)}, u32[]{:S(2)}, u32[]{:S(2)}) %collective-permute-start.31) | collective-permute-done | bytes 1048608 | tf_op jit(solution)/shard_map/ppermute | solution.py:466
  630.7 55.7 %psum.7 = f32[2,2048]{1,0:T(2,128)S(1)} all-reduce(f32[2,2048]{1,0:T(2,128)S(1)} %pad_maximum_fusion.8), channel_id=1, replica_groups=mesh['fsdp'=8,'tp'=4] {'fsdp','tp'}, use_global_device_ids=true, to_apply=%region_6.7 | all-reduce | flops 4096 | bytes 32768 | tf_op jit(solution)/shard_map/psum | solution.py:513
  687.8 5.2 fusion.20
  697.2 3.7 convert_add_fusion.5
  (275 shorter events, 166.3 us)
Async XLA Ops:
  0.7 45.9 %collective-permute-start.16 = (bf16[512,256]{1,0:T(8,128)(2,1)}, bf16[512,256]{1,0:T(8,128)(2,1)}, u32[]{:S(2)}, u32[]{:S(2)}) collective-permute-start(bf16[512,256]{1,0:T(8,128)(2,1)} %param.14), channel_id=1, source_target_pairs={{0,8},{4,12},{8,0},{12,4},{16,24},{20,28},{24,16},{28,20},{1,9},{5... | collective-permute-start | bytes 786440 | tf_op jit(solution)/shard_map/ppermute | solution.py:348
  3.7 37.5 %collective-permute-start.17 = (bf16[512,256]{1,0:T(8,128)(2,1)}, bf16[512,256]{1,0:T(8,128)(2,1)S(1)}, u32[]{:S(2)}, u32[]{:S(2)}) collective-permute-start(bf16[512,256]{1,0:T(8,128)(2,1)} %param.14), channel_id=1, source_target_pairs={{0,16},{4,20},{8,24},{12,28},{16,0},{20,4},{24,8},{28,12},{1,17},{... | collective-permute-start | bytes 786440 | tf_op jit(solution)/shard_map/ppermute | solution.py:348
  14.4 60.5 %collective-permute-start = (bf16[256,2048]{1,0:T(8,128)(2,1)}, bf16[256,2048]{1,0:T(8,128)(2,1)}, u32[]{:S(2)}, u32[]{:S(2)}) collective-permute-start(bf16[256,2048]{1,0:T(8,128)(2,1)} %constant_dynamic-update-slice_fusion), channel_id=1, source_target_pairs={{0,1},{1,2},{2,3},{4,5},{5,6},{6,7},{8,9},{9,10},{10,11},{12,13},{... | collective-permute-start | bytes 3145736 | tf_op jit(solution)/shard_map/ppermute | solution.py:440
  20.5 52.0 %collective-permute-start.6 = (bf16[256,1536]{1,0:T(8,128)(2,1)S(1)}, bf16[256,1536]{1,0:T(8,128)(2,1)}, u32[]{:S(2)}, u32[]{:S(2)}) collective-permute-start(bf16[256,1536]{1,0:T(8,128)(2,1)S(1)} %copy.26), channel_id=1, source_target_pairs={{0,8},{4,12},{8,0},{12,4},{16,24},{20,28},{24,16},{28,20},{1,9},{5... | collective-permute-start | bytes 2359304 | tf_op jit(solution)/shard_map/ppermute | solution.py:348
  21.1 54.4 %collective-permute-start.21 = (bf16[2048,256]{1,0:T(8,128)(2,1)}, bf16[2048,256]{1,0:T(8,128)(2,1)S(1)}, u32[]{:S(2)}, u32[]{:S(2)}) collective-permute-start(bf16[2048,256]{1,0:T(8,128)(2,1)} %param.16), channel_id=1, source_target_pairs={{0,8},{4,12},{8,0},{12,4},{16,24},{20,28},{24,16},{28,20},{1,9},{5... | collective-permute-start | bytes 3145736 | tf_op jit(solution)/shard_map/ppermute | solution.py:348
  41.2 29.0 %collective-permute-start.7 = (bf16[256,1536]{1,0:T(8,128)(2,1)S(1)}, bf16[256,1536]{1,0:T(8,128)(2,1)}, u32[]{:S(2)}, u32[]{:S(2)}) collective-permute-start(bf16[256,1536]{1,0:T(8,128)(2,1)S(1)} %copy.26), channel_id=1, source_target_pairs={{0,16},{4,20},{8,24},{12,28},{16,0},{20,4},{24,8},{28,12},{1,17},{... | collective-permute-start | bytes 2359304 | tf_op jit(solution)/shard_map/ppermute | solution.py:348
  69.6 26.3 %collective-permute-start.22 = (bf16[2048,256]{1,0:T(8,128)(2,1)}, bf16[2048,256]{1,0:T(8,128)(2,1)S(1)}, u32[]{:S(2)}, u32[]{:S(2)}) collective-permute-start(bf16[2048,256]{1,0:T(8,128)(2,1)} %param.16), channel_id=1, source_target_pairs={{0,16},{4,20},{8,24},{12,28},{16,0},{20,4},{24,8},{28,12},{1,17},{... | collective-permute-start | bytes 3145736 | tf_op jit(solution)/shard_map/ppermute | solution.py:348
  70.3 28.2 %collective-permute-start.1 = (bf16[256,2048]{1,0:T(8,128)(2,1)}, bf16[256,2048]{1,0:T(8,128)(2,1)S(1)}, u32[]{:S(2)}, u32[]{:S(2)}) collective-permute-start(bf16[256,2048]{1,0:T(8,128)(2,1)} %constant_dynamic-update-slice_fusion), channel_id=1, source_target_pairs={{1,0},{2,1},{3,2},{5,4},{6,5},{7,6},{9,8},{10,9},{11,10},{13,12},{... | collective-permute-start | bytes 3145736 | tf_op jit(solution)/shard_map/ppermute | solution.py:441
  72.6 43.7 %collective-permute-start.33 = (bf16[256,2048]{1,0:T(8,128)(2,1)}, bf16[256,2048]{1,0:T(8,128)(2,1)S(1)}, u32[]{:S(2)}, u32[]{:S(2)}) collective-permute-start(bf16[256,2048]{1,0:T(8,128)(2,1)} %constant_dynamic-update-slice_fusion.52), channel_id=1, source_target_pairs={{1,0},{2,1},{3,2},{5,4},{6,5},{7,6},{9,8},{10,9},{11,10},{13,12},{... | collective-permute-start | bytes 3145736 | tf_op jit(solution)/shard_map/ppermute | solution.py:441
  74.9 41.3 %collective-permute-start.11 = (bf16[256,2048]{1,0:T(8,128)(2,1)S(1)}, bf16[256,2048]{1,0:T(8,128)(2,1)S(1)}, u32[]{:S(2)}, u32[]{:S(2)}) collective-permute-start(bf16[256,2048]{1,0:T(8,128)(2,1)S(1)} %copy-done.8), channel_id=1, source_target_pairs={{0,8},{4,12},{8,0},{12,4},{16,24},{20,28},{24,16},{28,20},{1,9},{5... | collective-permute-start | bytes 3145736 | tf_op jit(solution)/shard_map/ppermute | solution.py:348
  75.5 42.3 %collective-permute-start.12 = (bf16[256,2048]{1,0:T(8,128)(2,1)S(1)}, bf16[256,2048]{1,0:T(8,128)(2,1)S(1)}, u32[]{:S(2)}, u32[]{:S(2)}) collective-permute-start(bf16[256,2048]{1,0:T(8,128)(2,1)S(1)} %copy-done.8), channel_id=1, source_target_pairs={{0,16},{4,20},{8,24},{12,28},{16,0},{20,4},{24,8},{28,12},{1,17},{... | collective-permute-start | bytes 3145736 | tf_op jit(solution)/shard_map/ppermute | solution.py:348
  95.9 24.9 %collective-permute-start.8 = (bf16[128,1536]{1,0:T(8,128)(2,1)S(1)}, bf16[128,1536]{1,0:T(8,128)(2,1)S(1)}, u32[]{:S(2)}, u32[]{:S(2)}) collective-permute-start(bf16[128,1536]{1,0:T(8,128)(2,1)S(1)} %slice.188), channel_id=1, source_target_pairs={{0,8},{4,12},{8,0},{12,4},{16,24},{20,28},{24,16},{28,20},{1,9},{5... | collective-permute-start | bytes 1179656 | tf_op jit(solution)/shard_map/ppermute | solution.py:348
  98.5 32.8 %collective-permute-start.32 = (bf16[256,2048]{1,0:T(8,128)(2,1)}, bf16[256,2048]{1,0:T(8,128)(2,1)S(1)}, u32[]{:S(2)}, u32[]{:S(2)}) collective-permute-start(bf16[256,2048]{1,0:T(8,128)(2,1)} %constant_dynamic-update-slice_fusion.52), channel_id=1, source_target_pairs={{0,1},{1,2},{2,3},{4,5},{5,6},{6,7},{8,9},{9,10},{10,11},{12,13},{... | collective-permute-start | bytes 3145736 | tf_op jit(solution)/shard_map/ppermute | solution.py:440
  117.8 27.9 %collective-permute-start.34 = (bf16[256,2048]{1,0:T(8,128)(2,1)S(1)}, bf16[256,2048]{1,0:T(8,128)(2,1)S(1)}, u32[]{:S(2)}, u32[]{:S(2)}) collective-permute-start(bf16[256,2048]{1,0:T(8,128)(2,1)S(1)} %collective-permute-done.33), channel_id=1, source_target_pairs={{1,0},{2,1},{5,4},{6,5},{9,8},{10,9},{13,12},{14,13},{17,16},{18,1... | collective-permute-start | bytes 3145736 | tf_op jit(solution)/shard_map/ppermute | solution.py:441
  127.8 19.3 %collective-permute-start.24 = (bf16[2048,128]{1,0:T(8,128)(2,1)S(1)}, bf16[2048,128]{1,0:T(8,128)(2,1)S(1)}, u32[]{:S(2)}, u32[]{:S(2)}) collective-permute-start(bf16[2048,128]{1,0:T(8,128)(2,1)S(1)} %slice.195), channel_id=1, source_target_pairs={{0,16},{4,20},{8,24},{12,28},{16,0},{20,4},{24,8},{28,12},{1,17},{... | collective-permute-start | bytes 1572872 | tf_op jit(solution)/shard_map/ppermute | solution.py:348
  131.8 36.4 %collective-permute-start.2 = (bf16[256,2048]{1,0:T(8,128)(2,1)S(1)}, bf16[256,2048]{1,0:T(8,128)(2,1)S(1)}, u32[]{:S(2)}, u32[]{:S(2)}) collective-permute-start(bf16[256,2048]{1,0:T(8,128)(2,1)S(1)} %collective-permute-done.1), channel_id=1, source_target_pairs={{1,0},{2,1},{5,4},{6,5},{9,8},{10,9},{13,12},{14,13},{17,16},{18,1... | collective-permute-start | bytes 3145736 | tf_op jit(solution)/shard_map/ppermute | solution.py:441
  135.6 32.6 %collective-permute-start.36 = (bf16[256,2048]{1,0:T(8,128)(2,1)S(1)}, bf16[256,2048]{1,0:T(8,128)(2,1)S(1)}, u32[]{:S(2)}, u32[]{:S(2)}) collective-permute-start(bf16[256,2048]{1,0:T(8,128)(2,1)S(1)} %collective-permute-done.32), channel_id=1, source_target_pairs={{1,2},{2,3},{5,6},{6,7},{9,10},{10,11},{13,14},{14,15},{17,18},{18... | collective-permute-start | bytes 3145736 | tf_op jit(solution)/shard_map/ppermute | solution.py:440
  145.7 44.9 %collective-permute-start.35 = (bf16[256,2048]{1,0:T(8,128)(2,1)S(1)}, bf16[256,2048]{1,0:T(8,128)(2,1)S(1)}, u32[]{:S(2)}, u32[]{:S(2)}) collective-permute-start(bf16[256,2048]{1,0:T(8,128)(2,1)S(1)} %collective-permute-done.34), channel_id=1, source_target_pairs={{1,0},{5,4},{9,8},{13,12},{17,16},{21,20},{25,24},{29,28}} | collective-permute-start | bytes 3145736 | tf_op jit(solution)/shard_map/ppermute | solution.py:441
  149.9 44.2 %collective-permute-start.4 = (bf16[256,2048]{1,0:T(8,128)(2,1)}, bf16[256,2048]{1,0:T(8,128)(2,1)S(1)}, u32[]{:S(2)}, u32[]{:S(2)}) collective-permute-start(bf16[256,2048]{1,0:T(8,128)(2,1)} %collective-permute-done), channel_id=1, source_target_pairs={{1,2},{2,3},{5,6},{6,7},{9,10},{10,11},{13,14},{14,15},{17,18},{18... | collective-permute-start | bytes 3145736 | tf_op jit(solution)/shard_map/ppermute | solution.py:440
  159.7 58.2 %collective-permute-start.10 = (bf16[1024,1536]{1,0:T(8,128)(2,1)}, bf16[1024,1536]{1,0:T(8,128)(2,1)}, u32[]{:S(2)}, u32[]{:S(2)}) collective-permute-start(bf16[1024,1536]{1,0:T(8,128)(2,1)} %get-tuple-element.104), channel_id=1, source_target_pairs={{0,4},{4,0},{8,12},{12,8},{16,20},{20,16},{24,28},{28,24},{1,5},{5... | collective-permute-start | bytes 9437192 | tf_op jit(solution)/shard_map/ppermute | solution.py:348
  168.2 152.3 %collective-permute-start.25 = (bf16[2048,1024]{1,0:T(8,128)(2,1)}, bf16[2048,1024]{1,0:T(8,128)(2,1)S(1)}, u32[]{:S(2)}, u32[]{:S(2)}) collective-permute-start(bf16[2048,1024]{1,0:T(8,128)(2,1)} %get-tuple-element.96), channel_id=1, source_target_pairs={{0,4},{4,0},{8,12},{12,8},{16,20},{20,16},{24,28},{28,24},{1,5},{5... | collective-permute-start | bytes 12582920 | tf_op jit(solution)/shard_map/ppermute | solution.py:348
  168.2 44.3 %collective-permute-start.3 = (bf16[256,2048]{1,0:T(8,128)(2,1)S(1)}, bf16[256,2048]{1,0:T(8,128)(2,1)}, u32[]{:S(2)}, u32[]{:S(2)}) collective-permute-start(bf16[256,2048]{1,0:T(8,128)(2,1)S(1)} %collective-permute-done.2), channel_id=1, source_target_pairs={{1,0},{5,4},{9,8},{13,12},{17,16},{21,20},{25,24},{29,28}} | collective-permute-start | bytes 3145736 | tf_op jit(solution)/shard_map/ppermute | solution.py:441
  194.1 104.3 %collective-permute-start.15 = (bf16[1024,2048]{1,0:T(8,128)(2,1)}, bf16[1024,2048]{1,0:T(8,128)(2,1)}, u32[]{:S(2)}, u32[]{:S(2)}) collective-permute-start(bf16[1024,2048]{1,0:T(8,128)(2,1)} %get-tuple-element.100), channel_id=1, source_target_pairs={{0,4},{4,0},{8,12},{12,8},{16,20},{20,16},{24,28},{28,24},{1,5},{5... | collective-permute-start | bytes 12582920 | tf_op jit(solution)/shard_map/ppermute | solution.py:348
  194.1 22.4 %collective-permute-start.5 = (bf16[256,2048]{1,0:T(8,128)(2,1)S(1)}, bf16[256,2048]{1,0:T(8,128)(2,1)}, u32[]{:S(2)}, u32[]{:S(2)}) collective-permute-start(bf16[256,2048]{1,0:T(8,128)(2,1)S(1)} %collective-permute-done.4), channel_id=1, source_target_pairs={{2,3},{6,7},{10,11},{14,15},{18,19},{22,23},{26,27},{30,31}} | collective-permute-start | bytes 3145736 | tf_op jit(solution)/shard_map/ppermute | solution.py:440
  255.3 23.3 %collective-permute-start.49 = (bf16[1024,512]{1,0:T(8,128)(2,1)}, bf16[1024,512]{1,0:T(8,128)(2,1)S(1)}, u32[]{:S(2)}, u32[]{:S(2)}) collective-permute-start(bf16[1024,512]{1,0:T(8,128)(2,1)} %out_grad_away.1), channel_id=1, source_target_pairs={{0,4},{4,0},{8,12},{12,8},{16,20},{20,16},{24,28},{28,24},{1,5},{5... | collective-permute-start | bytes 3145736 | tf_op jit(solution)/shard_map/ppermute | solution.py:348
  294.5 129.4 %collective-permute-start.44 = (bf16[1024,1536]{1,0:T(8,128)(2,1)}, bf16[1024,1536]{1,0:T(8,128)(2,1)}, u32[]{:S(2)}, u32[]{:S(2)}) collective-permute-start(bf16[1024,1536]{1,0:T(8,128)(2,1)} %qkv_grad_away.1), channel_id=1, source_target_pairs={{0,4},{4,0},{8,12},{12,8},{16,20},{20,16},{24,28},{28,24},{1,5},{5... | collective-permute-start | bytes 9437192 | tf_op jit(solution)/shard_map/ppermute | solution.py:348
  294.7 105.7 %collective-permute-start.53 = (bf16[256,512]{1,0:T(8,128)(2,1)S(1)}, bf16[256,512]{1,0:T(8,128)(2,1)S(1)}, u32[]{:S(2)}, u32[]{:S(2)}) collective-permute-start(bf16[256,512]{1,0:T(8,128)(2,1)S(1)} %pad_maximum_fusion.7), channel_id=1, source_target_pairs={{0,16},{4,20},{8,24},{12,28},{16,0},{20,4},{24,8},{28,12},{1,17},{... | collective-permute-start | bytes 786440 | tf_op jit(solution)/shard_map/ppermute | solution.py:348
  297.0 103.4 %collective-permute-start.51 = (bf16[256,512]{1,0:T(8,128)(2,1)}, bf16[256,512]{1,0:T(8,128)(2,1)S(1)}, u32[]{:S(2)}, u32[]{:S(2)}) collective-permute-start(bf16[256,512]{1,0:T(8,128)(2,1)} %pad_maximum_fusion.6), channel_id=1, source_target_pairs={{0,8},{4,12},{8,0},{12,4},{16,24},{20,28},{24,16},{28,20},{1,9},{5... | collective-permute-start | bytes 786440 | tf_op jit(solution)/shard_map/ppermute | solution.py:348
  360.9 41.1 %collective-permute-start.38 = (bf16[256,2048]{1,0:T(8,128)(2,1)S(1)}, bf16[256,2048]{1,0:T(8,128)(2,1)}, u32[]{:S(2)}, u32[]{:S(2)}) collective-permute-start(bf16[256,2048]{1,0:T(8,128)(2,1)S(1)} %constant_dynamic-slice_fusion.1), channel_id=1, source_target_pairs={{0,1},{4,5},{8,9},{12,13},{16,17},{20,21},{24,25},{28,29}} | collective-permute-start | bytes 3145736 | tf_op jit(solution)/shard_map/ppermute | solution.py:465
  380.7 27.3 %collective-permute-start.26 = (bf16[256,2048]{1,0:T(8,128)(2,1)S(1)}, bf16[256,2048]{1,0:T(8,128)(2,1)}, u32[]{:S(2)}, u32[]{:S(2)}) collective-permute-start(bf16[256,2048]{1,0:T(8,128)(2,1)S(1)} %constant_dynamic-slice_fusion.3), channel_id=1, source_target_pairs={{0,1},{4,5},{8,9},{12,13},{16,17},{20,21},{24,25},{28,29}} | collective-permute-start | bytes 3145736 | tf_op jit(solution)/shard_map/ppermute | solution.py:465
  400.4 149.8 %collective-permute-start.54 = (bf16[1024,2048]{1,0:T(8,128)(2,1)}, bf16[1024,2048]{1,0:T(8,128)(2,1)}, u32[]{:S(2)}, u32[]{:S(2)}) collective-permute-start(bf16[1024,2048]{1,0:T(8,128)(2,1)} %up_grad_away.1), channel_id=1, source_target_pairs={{0,4},{4,0},{8,12},{12,8},{16,20},{20,16},{24,28},{28,24},{1,5},{5... | collective-permute-start | bytes 12582920 | tf_op jit(solution)/shard_map/ppermute | solution.py:348
  400.4 162.5 %collective-permute-start.59 = (bf16[1024,2048]{1,0:T(8,128)(2,1)}, bf16[1024,2048]{1,0:T(8,128)(2,1)}, u32[]{:S(2)}, u32[]{:S(2)}) collective-permute-start(bf16[1024,2048]{1,0:T(8,128)(2,1)} %down_grad_away.1), channel_id=1, source_target_pairs={{0,4},{4,0},{8,12},{12,8},{16,20},{20,16},{24,28},{28,24},{1,5},{5... | collective-permute-start | bytes 12582920 | tf_op jit(solution)/shard_map/ppermute | solution.py:348
  404.9 29.2 %collective-permute-start.39 = (bf16[256,2048]{1,0:T(8,128)(2,1)}, bf16[256,2048]{1,0:T(8,128)(2,1)S(1)}, u32[]{:S(2)}, u32[]{:S(2)}) collective-permute-start(bf16[256,2048]{1,0:T(8,128)(2,1)} %fusion.2), channel_id=1, source_target_pairs={{0,1},{1,2},{4,5},{5,6},{8,9},{9,10},{12,13},{13,14},{16,17},{17,1... | collective-permute-start | bytes 3145736 | tf_op jit(solution)/shard_map/ppermute | solution.py:465
  409.9 42.5 %collective-permute-start.27 = (bf16[256,2048]{1,0:T(8,128)(2,1)S(1)}, bf16[256,2048]{1,0:T(8,128)(2,1)S(1)}, u32[]{:S(2)}, u32[]{:S(2)}) collective-permute-start(bf16[256,2048]{1,0:T(8,128)(2,1)S(1)} %fusion), channel_id=1, source_target_pairs={{0,1},{1,2},{4,5},{5,6},{8,9},{9,10},{12,13},{13,14},{16,17},{17,1... | collective-permute-start | bytes 3145736 | tf_op jit(solution)/shard_map/ppermute | solution.py:465
  433.5 21.3 %collective-permute-start.45 = (bf16[128,1536]{1,0:T(8,128)(2,1)S(1)}, bf16[128,1536]{1,0:T(8,128)(2,1)S(1)}, u32[]{:S(2)}, u32[]{:S(2)}) collective-permute-start(bf16[128,1536]{1,0:T(8,128)(2,1)S(1)} %get-tuple-element.67), channel_id=1, source_target_pairs={{0,16},{4,20},{8,24},{12,28},{16,0},{20,4},{24,8},{28,12},{1,17},{... | collective-permute-start | bytes 1179656 | tf_op jit(solution)/shard_map/ppermute | solution.py:348
  434.1 21.5 %collective-permute-start.47 = (bf16[128,1536]{1,0:T(8,128)(2,1)S(1)}, bf16[128,1536]{1,0:T(8,128)(2,1)S(1)}, u32[]{:S(2)}, u32[]{:S(2)}) collective-permute-start(bf16[128,1536]{1,0:T(8,128)(2,1)S(1)} %get-tuple-element.66), channel_id=1, source_target_pairs={{0,8},{4,12},{8,0},{12,4},{16,24},{20,28},{24,16},{28,20},{1,9},{5... | collective-permute-start | bytes 1179656 | tf_op jit(solution)/shard_map/ppermute | solution.py:348
  455.9 19.1 %collective-permute-start.48 = (bf16[256,1536]{1,0:T(8,128)(2,1)S(1)}, bf16[256,1536]{1,0:T(8,128)(2,1)S(1)}, u32[]{:S(2)}, u32[]{:S(2)}) collective-permute-start(bf16[256,1536]{1,0:T(8,128)(2,1)S(1)} %pad_maximum_fusion.5), channel_id=1, source_target_pairs={{0,16},{4,20},{8,24},{12,28},{16,0},{20,4},{24,8},{28,12},{1,17},{... | collective-permute-start | bytes 2359304 | tf_op jit(solution)/shard_map/ppermute | solution.py:348
  456.5 34.0 %collective-permute-start.46 = (bf16[256,1536]{1,0:T(8,128)(2,1)S(1)}, bf16[256,1536]{1,0:T(8,128)(2,1)S(1)}, u32[]{:S(2)}, u32[]{:S(2)}) collective-permute-start(bf16[256,1536]{1,0:T(8,128)(2,1)S(1)} %pad_maximum_fusion.4), channel_id=1, source_target_pairs={{0,8},{4,12},{8,0},{12,4},{16,24},{20,28},{24,16},{28,20},{1,9},{5... | collective-permute-start | bytes 2359304 | tf_op jit(solution)/shard_map/ppermute | solution.py:348
  458.5 36.0 %collective-permute-start.42 = (bf16[256,2048]{1,0:T(8,128)(2,1)}, bf16[256,2048]{1,0:T(8,128)(2,1)}, u32[]{:S(2)}, u32[]{:S(2)}) collective-permute-start(bf16[256,2048]{1,0:T(8,128)(2,1)} %fusion.3), channel_id=1, source_target_pairs={{3,2},{2,1},{7,6},{6,5},{11,10},{10,9},{15,14},{14,13},{19,18},{18... | collective-permute-start | bytes 3145736 | tf_op jit(solution)/shard_map/ppermute | solution.py:466
  474.9 117.9 %collective-permute-start.40 = (bf16[256,2048]{1,0:T(8,128)(2,1)}, bf16[256,2048]{1,0:T(8,128)(2,1)}, u32[]{:S(2)}, u32[]{:S(2)}) collective-permute-start(bf16[256,2048]{1,0:T(8,128)(2,1)} %get-tuple-element.48), channel_id=1, source_target_pairs={{0,1},{1,2},{2,3},{4,5},{5,6},{6,7},{8,9},{9,10},{10,11},{12,13},{... | collective-permute-start | bytes 3145736 | tf_op jit(solution)/shard_map/ppermute | solution.py:465
  490.5 56.5 %collective-permute-start.30 = (bf16[256,2048]{1,0:T(8,128)(2,1)}, bf16[256,2048]{1,0:T(8,128)(2,1)}, u32[]{:S(2)}, u32[]{:S(2)}) collective-permute-start(bf16[256,2048]{1,0:T(8,128)(2,1)} %fusion.1), channel_id=1, source_target_pairs={{3,2},{2,1},{7,6},{6,5},{11,10},{10,9},{15,14},{14,13},{19,18},{18... | collective-permute-start | bytes 3145736 | tf_op jit(solution)/shard_map/ppermute | solution.py:466
  494.5 109.6 %collective-permute-start.28 = (bf16[256,2048]{1,0:T(8,128)(2,1)S(1)}, bf16[256,2048]{1,0:T(8,128)(2,1)S(1)}, u32[]{:S(2)}, u32[]{:S(2)}) collective-permute-start(bf16[256,2048]{1,0:T(8,128)(2,1)S(1)} %copy-done.9), channel_id=1, source_target_pairs={{0,1},{1,2},{2,3},{4,5},{5,6},{6,7},{8,9},{9,10},{10,11},{12,13},{... | collective-permute-start | bytes 3145736 | tf_op jit(solution)/shard_map/ppermute | solution.py:465
  547.0 47.4 %collective-permute-start.43 = (bf16[256,2048]{1,0:T(8,128)(2,1)S(1)}, bf16[256,2048]{1,0:T(8,128)(2,1)S(1)}, u32[]{:S(2)}, u32[]{:S(2)}) collective-permute-start(bf16[256,2048]{1,0:T(8,128)(2,1)S(1)} %add_convert_fusion), channel_id=1, source_target_pairs={{3,2},{2,1},{1,0},{7,6},{6,5},{5,4},{11,10},{10,9},{9,8},{15,14},{... | collective-permute-start | bytes 3145736 | tf_op jit(solution)/shard_map/ppermute | solution.py:466
  586.1 37.7 %collective-permute-start.31 = (bf16[256,2048]{1,0:T(8,128)(2,1)S(1)}, bf16[256,2048]{1,0:T(8,128)(2,1)S(1)}, u32[]{:S(2)}, u32[]{:S(2)}) collective-permute-start(bf16[256,2048]{1,0:T(8,128)(2,1)S(1)} %add_convert_fusion.2), channel_id=1, source_target_pairs={{3,2},{2,1},{1,0},{7,6},{6,5},{5,4},{11,10},{10,9},{9,8},{15,14},{... | collective-permute-start | bytes 3145736 | tf_op jit(solution)/shard_map/ppermute | solution.py:466
  587.4 109.7 %collective-permute-start.58 = (bf16[256,2048]{1,0:T(8,128)(2,1)}, bf16[256,2048]{1,0:T(8,128)(2,1)}, u32[]{:S(2)}, u32[]{:S(2)}) collective-permute-start(bf16[256,2048]{1,0:T(8,128)(2,1)} %pad_maximum_fusion.1), channel_id=1, source_target_pairs={{0,16},{4,20},{8,24},{12,28},{16,0},{20,4},{24,8},{28,12},{1,17},{... | collective-permute-start | bytes 3145736 | tf_op jit(solution)/shard_map/ppermute | solution.py:348
  592.8 104.3 %collective-permute-start.56 = (bf16[256,2048]{1,0:T(8,128)(2,1)}, bf16[256,2048]{1,0:T(8,128)(2,1)}, u32[]{:S(2)}, u32[]{:S(2)}) collective-permute-start(bf16[256,2048]{1,0:T(8,128)(2,1)} %pad_maximum_fusion), channel_id=1, source_target_pairs={{0,8},{4,12},{8,0},{12,4},{16,24},{20,28},{24,16},{28,20},{1,9},{5... | collective-permute-start | bytes 3145736 | tf_op jit(solution)/shard_map/ppermute | solution.py:348
  594.3 98.6 %collective-permute-start.63 = (bf16[256,2048]{1,0:T(8,128)(2,1)}, bf16[256,2048]{1,0:T(8,128)(2,1)}, u32[]{:S(2)}, u32[]{:S(2)}) collective-permute-start(bf16[256,2048]{1,0:T(8,128)(2,1)} %pad_maximum_fusion.3), channel_id=1, source_target_pairs={{0,16},{4,20},{8,24},{12,28},{16,0},{20,4},{24,8},{28,12},{1,17},{... | collective-permute-start | bytes 3145736 | tf_op jit(solution)/shard_map/ppermute | solution.py:348
  604.1 88.8 %collective-permute-start.61 = (bf16[256,2048]{1,0:T(8,128)(2,1)}, bf16[256,2048]{1,0:T(8,128)(2,1)}, u32[]{:S(2)}, u32[]{:S(2)}) collective-permute-start(bf16[256,2048]{1,0:T(8,128)(2,1)} %pad_maximum_fusion.2), channel_id=1, source_target_pairs={{0,8},{4,12},{8,0},{12,4},{16,24},{20,28},{24,16},{28,20},{1,9},{5... | collective-permute-start | bytes 3145736 | tf_op jit(solution)/shard_map/ppermute | solution.py:348
  (37 other events, 306.6 us)
